TPU v7x, 256 devices: a whole 4x4x8 slice. The times are simulated.
256 devices in a mesh: dp: 32 (over z_lo, y, core), st: 8 (over x, z_hi).
Axes of the slice: x: 4, y: 4, z: 8 (z_hi: 2, z_lo: 4; z = z_hi * 4 + z_lo), core: 2. Of those that a mesh axis runs over, the one named last changes fastest.
Arguments:
- hidden: bfloat16 [32768, 3584], P(('dp', 'st')), may hold values from -12 to 12, as said below
- w_down: bfloat16 [3584, 1536], P(None, 'st')
- norm_gain: float32 [1536], P('st'), may hold values from 0.5 to 1.5
- w_up: bfloat16 [1536, 12288], P(None, 'st'), may hold values from -0.15625 to 0.15625
- grad_query: bfloat16 [32768, 12288], P('dp', 'st'), may hold values from -0.078125 to 0.078125
Outputs:
- grad_down: float32 [3584, 1536], P('dp', 'st')
- grad_up: float32 [1536, 12288], P('dp', 'st')
- grad_gain: float32 [1536], P('st')
Inputs may be any that keep to these rules, and one draw needn't show every extreme that they name: hidden states of order one.
All inputs are finite; a program needn't handle non-finite values.
Results may differ from a plain program's by a relative error of at most 0.0029.
Values may be sent and summed in bfloat16 or wider, within the bound.
A program may use at most 128 MiB of HBM per device.

v0:
```python
import jax
import jax.numpy as jnp
from jax import lax
from jax.sharding import PartitionSpec as P

L = 1536


def local(hidden, w_down, norm_gain, w_up, grad_query):
    gathered = lax.all_gather(hidden, "st", axis=0, tiled=True)
    latent = jnp.dot(gathered, w_down, preferred_element_type=jnp.float32)
    square_part = jnp.sum(latent * latent, axis=1, keepdims=True)
    summed = lax.psum(square_part, "st")
    inverse = lax.rsqrt(summed / L + 1e-06)
    normed_part = (latent * inverse * norm_gain).astype(jnp.bfloat16)
    normed = lax.all_gather(normed_part, "st", axis=1, tiled=True)
    picked = normed
    grad_up = lax.psum_scatter(
        lax.dot_general(
            picked, grad_query, (((0,), (0,)), ((), ())), preferred_element_type=jnp.float32
        ),
        "dp",
        scatter_dimension=0,
        tiled=True,
    )
    term_normed = lax.dot_general(
        grad_query, w_up, (((1,), (1,)), ((), ())), preferred_element_type=jnp.float32
    )
    grad_normed = lax.psum_scatter(term_normed, "st", scatter_dimension=1, tiled=True)
    inner_part = jnp.sum(norm_gain * grad_normed * latent, axis=1, keepdims=True)
    inner = lax.psum(inner_part, "st")
    grad_latent = (inverse * norm_gain * grad_normed - latent * inverse**3 * inner / L).astype(
        jnp.bfloat16
    )
    picked = gathered
    grad_down = lax.psum_scatter(
        lax.dot_general(
            picked, grad_latent, (((0,), (0,)), ((), ())), preferred_element_type=jnp.float32
        ),
        "dp",
        scatter_dimension=0,
        tiled=True,
    )
    gain_part = jnp.sum(grad_normed * latent * inverse, axis=0)
    grad_gain = lax.psum(gain_part, "dp")
    return (grad_down, grad_up, grad_gain)


def solution(mesh):
    placed = (P(("dp", "st"), None), P(None, "st"), P("st"), P(None, "st"), P("dp", "st"))
    return jax.shard_map(
        local,
        mesh=mesh,
        in_specs=placed,
        out_specs=(P("dp", "st"), P("dp", "st"), P("st")),
        check_vma=False,
    )
```

profile of v0, /device:TPU:1, one launch (start us, length us, event | category | flops | bytes accessed | tf_op | source)
XLA Modules:
  0.0 723.5 jit_solution(9971653620235852345)
XLA Ops:
  7.2 0.0 copy-start
  7.2 0.0 all-gather.3.cloned.1.call-start
  7.2 0.7 all-gather.3.cloned.1.call-update
  7.9 0.0 reduce-scatter.6.cloned.1.call-start
  8.0 1.1 copy-done
  9.1 9.4 %fusion.6 = f32[1024,1536]{0,1:T(8,128)} fusion(bf16[1024,1536]{1,0:T(8,128)(2,1)S(1)} %copy-done, bf16[1536,1536]{1,0:T(8,128)(2,1)} %param.8), kind=kOutput, calls=%fused_computation.14 | convolution fusion | flops 4831838208 | bytes 14155776 | tf_op jit(solution)/shard_map/dot_general | solution.py:26
  18.4 0.0 reduce-scatter.6.cloned.1.call-update
  18.4 0.0 copy-start.1
  18.5 0.0 all-gather.5.cloned.1.call-start
  18.5 152.1 %all-gather.3.cloned.1.call-done = bf16[1024,3584]{1,0:T(8,128)(2,1)} async-done(((bf16[128,3584]{1,0:T(8,128)(2,1)}), bf16[1024,3584]{1,0:T(8,128)(2,1)}) %all-gather.3.cloned.1.call-update) | async-done | bytes 7340048 | tf_op jit(solution)/shard_map/all_gather | solution.py:10
  170.6 6.8 multiply_reduce_fusion.2
  177.5 20.8 %psum.21 = f32[1024,1]{0,1:T(1,128)S(1)} all-reduce(f32[1024,1]{0,1:T(1,128)S(1)} %bitcast.16), channel_id=1, replica_groups=mesh['dp'=32,'st'=8] {'st'}, use_global_device_ids=true, to_apply=%region_1.0 | all-reduce | flops 1024 | bytes 8192 | tf_op jit(solution)/shard_map/psum | solution.py:13
  198.3 125.9 %reduce-scatter.6.cloned.1.call-done = f32[1024,192]{0,1:T(8,128)} async-done(((f32[1024,1536]{0,1:T(8,128)}), f32[1024,192]{0,1:T(8,128)}) %reduce-scatter.6.cloned.1.call-update) | async-done | bytes 786448 | tf_op jit(solution)/shard_map/reduce_scatter | solution.py:29
  324.2 0.0 copy-done.1
  324.2 2.3 multiply_reduce_fusion
  326.5 0.0 all-gather.5.cloned.1.call-update
  326.5 0.0 reduce-scatter.10.cloned.1.call-start
  326.6 20.4 %psum.22 = f32[1024]{0:T(1024)S(1)} all-reduce(f32[1024]{0:T(1024)S(1)} %get-tuple-element.4), channel_id=1, replica_groups=mesh['dp'=32,'st'=8] {'st'}, use_global_device_ids=true, to_apply=%region_4.0 | all-reduce | flops 1024 | bytes 8192 | tf_op jit(solution)/shard_map/psum | solution.py:31
  347.0 6.9 convolution_bitcast_fusion
  353.9 4.7 copy.8
  358.6 0.0 reduce-scatter.10.cloned.1.call-update
  358.6 0.0 reduce-scatter.8.cloned.1.call-start
  358.7 57.5 %all-gather.5.cloned.1.call-done = bf16[1024,1536]{0,1:T(8,128)(2,1)} async-done(((bf16[1024,192]{0,1:T(8,128)(2,1)}), bf16[1024,1536]{0,1:T(8,128)(2,1)}) %all-gather.5.cloned.1.call-update) | async-done | bytes 3145744 | tf_op jit(solution)/shard_map/all_gather | solution.py:16
  416.2 9.4 %fusion.7 = f32[1536,1536]{1,0:T(8,128)} fusion(bf16[1024,1536]{0,1:T(8,128)(2,1)} %all-gather.5.cloned.1.call-done, bf16[1024,1536]{1,0:T(8,128)(2,1)S(1)} %copy-done), kind=kOutput, calls=%fused_computation.15 | convolution fusion | flops 4831838208 | bytes 15728640 | tf_op jit(solution)/shard_map/dot_general | solution.py:19
  425.5 0.0 reduce-scatter.8.cloned.1.call-update
  425.5 68.4 %psum.23 = f32[192]{0:T(256)} all-reduce(f32[192]{0:T(256)S(1)} %get-tuple-element.3), channel_id=1, replica_groups=mesh['dp'=32,'st'=8] {'dp'}, use_global_device_ids=true, to_apply=%region_8.0 | all-reduce | flops 192 | bytes 1536 | tf_op jit(solution)/shard_map/psum | solution.py:45
  494.0 64.8 %reduce-scatter.10.cloned.1.call-done = f32[112,192]{1,0:T(8,128)} async-done(((f32[3584,192]{1,0:T(8,128)}), f32[112,192]{1,0:T(8,128)}) %reduce-scatter.10.cloned.1.call-update) | async-done | bytes 86032
  558.8 1.6 copy.9
  560.4 156.5 %reduce-scatter.8.cloned.1.call-done = f32[48,1536]{1,0:T(8,128)} async-done(((f32[1536,1536]{1,0:T(8,128)}), f32[48,1536]{1,0:T(8,128)}) %reduce-scatter.8.cloned.1.call-update) | async-done | bytes 294928 | tf_op jit(solution)/shard_map/reduce_scatter | solution.py:18
  (1 shorter events, 0.0 us)
Async XLA Ops:
  7.2 1.9 copy-start
  7.2 163.5 %all-gather.3.cloned.1.call-start = ((), (), s32[]{:S(2)}) async-start(), calls=%async_computation.3 | async-start | bytes 8257536 | tf_op jit(solution)/shard_map/all_gather | solution.py:10
  7.9 316.3 %reduce-scatter.6.cloned.1.call-start = ((), (), s32[]{:S(2)}) async-start(), calls=%async_computation.4 | async-start | bytes 7077888 | tf_op jit(solution)/shard_map/reduce_scatter | solution.py:29
  18.4 305.7 %copy-start.1 = (f32[192]{0:T(256)S(1)}, f32[192]{0:T(256)}, u32[]{:S(2)}) copy-start(f32[192]{0:T(256)} %param.7) | copy-start | bytes 2308
  18.5 397.7 %all-gather.5.cloned.1.call-start = ((), (), s32[]{:S(2)}) async-start(), calls=%async_computation.5 | async-start | bytes 3538944 | tf_op jit(solution)/shard_map/all_gather | solution.py:16
  326.5 232.3 %reduce-scatter.10.cloned.1.call-start = ((), (), s32[]{:S(2)}) async-start(), calls=%async_computation.7 | async-start | bytes 3784704
  358.6 358.3 %reduce-scatter.8.cloned.1.call-start = ((), (), s32[]{:S(2)}) async-start(), calls=%async_computation.6 | async-start | bytes 9732096 | tf_op jit(solution)/shard_map/reduce_scatter | solution.py:18
Sparse Core Ops, SparseCore 0:
  10.6 159.9 all-gather.2
  174.8 149.3 reduce-scatter.5
  327.1 88.9 all-gather.4
  418.7 140.0 reduce-scatter.9
  561.8 155.1 reduce-scatter.7
where the time goes:
time: 729 us; the launch traced here: 723 us
  waiting for transfers between devices  558 us (77%)
  blocking collectives  110 us (15%)
  matrix products  32.4 us (4%)
  between operations  13.8 us (2%)
  local copies, waits for them, and re-layouts  7.49 us (1%)
    reduce_scatter x1, waiting for transfers between devices, local(): lax.psum_scatter(lax.dot_general(picked, grad_query, (((0,), (0,)), ((),...  157 us
    all_gather x1, waiting for transfers between devices, local(): gathered = lax.all_gather(hidden, 'st', axis=0, tiled=True)  152 us
    reduce_scatter x1, waiting for transfers between devices, local(): lax.psum_scatter(term_normed, 'st', scatter_dimension=1, tiled=True)  126 us
    psum x1, blocking collectives, local(): grad_gain = lax.psum(gain_part, 'dp')  68.4 us
    unnamed x6, waiting for transfers between devices  65.6 us
    all_gather x1, waiting for transfers between devices, local(): normed = lax.all_gather(normed_part, 'st', axis=1, tiled=True)  57.5 us
    psum x1, blocking collectives, local(): summed = lax.psum(square_part, 'st')  20.8 us
    psum x1, blocking collectives, local(): inner = lax.psum(inner_part, 'st')  20.4 us
  transfers between devices with their start and end apart: 5, of which 5 were waited for; matrix products, arithmetic and copies ran while one was open for 5% of the time, Pallas kernels for 0%

commit v1 on v0

v1 whole, which is shorter than its diff:
```python
import functools

import jax
import jax.numpy as jnp
from jax import lax
from jax.experimental import pallas as pl
from jax.experimental.pallas import tpu as pltpu
from jax.sharding import PartitionSpec as P

L = 1536
MESH = pl.DeviceIdType.MESH
F32 = jnp.float32
BF16 = jnp.bfloat16
SUB = 112


def coordinates():
    dp = lax.axis_index("dp")
    st = lax.axis_index("st")
    zl, y, c = dp // 8, lax.rem(dp // 2, 4), lax.rem(dp, 2)
    x, zh = st // 2, lax.rem(st, 2)
    return x, y, zh * 4 + zl, c


def device(x, y, z, c):
    x, y, z, c = lax.rem(x + 8, 4), lax.rem(y + 8, 4), lax.rem(z + 16, 8), lax.rem(c + 2, 2)
    return ((lax.rem(z, 4) * 4 + y) * 2 + c, x * 2 + z // 4)


def send(src, dst, send_sem, recv_sem, to):
    copy = pltpu.make_async_remote_copy(
        src_ref=src, dst_ref=dst, send_sem=send_sem, recv_sem=recv_sem, device_id=to, device_id_type=MESH
    )
    copy.start()
    return copy


def meet(peers):
    barrier = pltpu.get_barrier_semaphore()
    for peer in peers:
        pl.semaphore_signal(barrier, inc=1, device_id=peer, device_id_type=MESH)
    pl.semaphore_wait(barrier, len(peers))


def front(
    hid, wd, gain, wup, gq, nt_out, gl_out, gp_out, ht_out,
    hk, xb, gb, w, snd, rcv, own, zs, zr, lp, lx, nat,
    loc_sem, x_s, x_r, g_s, g_r, h_s, h_r, n_s, n_r, q_s, q_r,
    za_s, za_r, zb_s, zb_r, yp_s, yp_r, ym_s, ym_r, yf_s, yf_r, l_s, l_r,
):
    x, y, z, c = coordinates()
    zh, zl = z // 4, lax.rem(z, 4)
    st = x * 2 + zh
    st_peers = [(dx, dz) for dz in (0, 4) for dx in (0, 1, 2, 3) if (dx, dz) != (0, 0)]
    s = 1 - 2 * c
    core_peer = device(x, y, z, c + 1)
    up_z, down_z = device(x, y, z + s, c), device(x, y, z - s, c)
    up_y, down_y = device(x, y + 1, z, c), device(x, y - 1, z, c)
    meet(
        [device(x + dx, y, z + dz, c) for dx, dz in st_peers] + [core_peer, up_z, down_z, up_y, down_y]
    )
    sends = []
    row = pl.multiple_of(c * 1792 + (y * 4 + zl) * SUB, 16)
    piece = wd.at[pl.ds(row, SUB)]
    own_piece = pltpu.make_async_copy(piece, xb.at[x], loc_sem.at[0])
    own_piece.start()
    x_copies = [
        send(piece, xb.at[x], x_s.at[d - 1], x_r.at[d - 1], device(x + d, y, z, c)) for d in (2, 1, 3)
    ]
    other_k = hid.at[:, pl.ds(pl.multiple_of((1 - c) * 1792, 128), 1792)]
    own_k = hid.at[:, pl.ds(pl.multiple_of(c * 1792, 128), 1792)]
    h_copy = send(other_k, hk.at[c], h_s, h_r, core_peer)
    own_hid = pltpu.make_async_copy(own_k, hk.at[c], loc_sem.at[1])
    own_hid.start()
    own_gain = pltpu.make_async_copy(gain, gb.at[st], loc_sem.at[2])
    own_gain.start()
    g_copies = [
        send(gain, gb.at[st], g_s.at[i], g_r.at[i], device(x + dx, y, z + dz, c))
        for i, (dx, dz) in enumerate(st_peers)
    ]
    sends += x_copies + [h_copy] + g_copies

    def cotangent(owner, store):
        def tile(i, _):
            cols = pl.ds(pl.multiple_of(i * 256, 256), 256)
            store(
                cols,
                lax.dot_general(
                    gq[pl.ds(pl.multiple_of(owner * 256, 256), 256), :],
                    wup[cols, :],
                    (((1,), (1,)), ((), ())),
                    preferred_element_type=F32,
                ),
            )
            return 0

        lax.fori_loop(0, 6, tile, 0)

    far = pl.ds(pl.multiple_of((1 - zh) * 128, 128), 128)
    near = pl.ds(pl.multiple_of(zh * 128, 128), 128)
    n_copies = {}

    def partial_for(j, d):
        def store(cols, value):
            snd[j, :, cols] = value.astype(BF16)

        cotangent(lax.rem(x + d, 4), store)
        n_copies[j, 0] = send(
            snd.at[j, far], rcv.at[j, far], n_s.at[j, 0], n_r.at[j, 0], device(x + d, y, z, c)
        )

    partial_for(0, 2)

    own_piece.wait()
    for copy in x_copies:
        copy.wait_recv()

    def unit(zz, yy):
        zz, yy = lax.rem(zz + 16, 8), lax.rem(yy + 8, 4)
        rows = pl.multiple_of((yy * 4 + lax.rem(zz, 4)) * SUB, 16)
        return w.at[zz // 4, pl.ds(rows, SUB)]

    my_rows = pl.ds(pl.multiple_of((y * 4 + zl) * SUB, 16), SUB)
    for i in range(4):
        w[zh, my_rows, i * 192 : (i + 1) * 192] = xb[i]

    owners = [z, z - s, z + s, z - 2 * s, z + 2 * s, z - 3 * s, z + 3 * s, z - 4 * s]
    za, zb, yp, ym, yf = {}, {}, {}, {}, {}

    def pass_on(k):
        here = unit(owners[k], y)
        if k == 0 or (k % 2 == 1 and k < 7):
            i = (k + 1) // 2
            za[i] = send(here, here, za_s.at[i], za_r.at[i], up_z)
        if k == 0 or (k % 2 == 0 and k < 6):
            i = k // 2
            zb[i] = send(here, here, zb_s.at[i], zb_r.at[i], down_z)
        yp[k] = send(here, here, yp_s.at[k], yp_r.at[k], up_y)
        ym[k] = send(here, here, ym_s.at[k], ym_r.at[k], down_y)

    def forward(k):
        yp[k].wait_recv()
        ym[k].wait_recv()
        if k % 2 == 0:
            there = unit(owners[k], y - 1)
            yf[k] = send(there, there, yf_s.at[k], yf_r.at[k], up_y)
        else:
            there = unit(owners[k], y + 1)
            yf[k] = send(there, there, yf_s.at[k], yf_r.at[k], down_y)

    pass_on(0)
    partial_for(1, 1)
    partial_for(2, 3)
    for j, d in enumerate((2, 1, 3)):
        n_copies[j, 1] = send(
            snd.at[j, near], rcv.at[j, near], n_s.at[j, 1], n_r.at[j, 1], device(x + d, y, z, c)
        )

    def keep(cols, value):
        own[:, cols] = value

    za[0].wait_recv()
    pass_on(1)
    zb[0].wait_recv()
    pass_on(2)
    cotangent(x, keep)

    def turn(i, _):
        cols = pl.ds(pl.multiple_of(i * 128, 128), 128)
        ht_out[cols, :] = hid[:, cols].astype(F32).T.astype(BF16)
        return 0

    lax.fori_loop(0, 28, turn, 0)
    forward(0)
    q_copy = None
    for k in range(3, 8):
        if k % 2 == 1:
            za[k // 2].wait_recv()
        else:
            zb[k // 2 - 1].wait_recv()
        pass_on(k)
        forward(k - 2)
        if k == 5:
            for j in range(3):
                n_copies[j, 0].wait_recv()
            total = own[far, :]
            for j in range(3):
                total = total + rcv[j, far, :].astype(F32)
            zs[...] = total.astype(zs.dtype)
            q_copy = send(zs, zr, q_s, q_r, device(x, y, z + 4, c))
    forward(6)
    forward(7)
    for k in range(8):
        yf[k].wait_recv()
    h_copy.wait_recv()
    own_hid.wait()

    for half in range(2):

        def tile(i, _):
            cols = pl.ds(pl.multiple_of(i * 256, 256), 256)
            value = jnp.dot(
                hk[...].reshape(256, 1792), w[half, :, cols], preferred_element_type=F32
            )
            lp[:, half, :, cols] = value.reshape(2, 128, 256)
            return 0

        lax.fori_loop(0, 3, tile, 0)
    l_copy = send(lp.at[1 - c], lx, l_s, l_r, core_peer)

    own_gain.wait()
    for copy in g_copies:
        copy.wait_recv()
    for j in range(3):
        n_copies[j, 1].wait_recv()
    q_copy.wait_recv()
    l_copy.wait_recv()
    for half in range(2):
        for i in range(4):
            piece_cols = pl.ds(i * 192, 192)
            at = i * 384 + half * 192
            nat[:, at : at + 192] = lp[c, half, :, piece_cols] + lx[half, :, piece_cols]
    for i in range(8):
        gp_out[:, i * 192 : (i + 1) * 192] = jnp.broadcast_to(gb[i], (8, 192))
    gains = gp_out[0:1, :]
    latent = nat[...]
    inverse = lax.rsqrt(jnp.sum(latent * latent, axis=1, keepdims=True) / L + 1e-06)
    total = own[near, :] + zr[...].astype(F32)
    for j in range(3):
        total = total + rcv[j, near, :].astype(F32)
    own[0:128, :] = total
    inner = jnp.sum(gains * total * latent, axis=1, keepdims=True)
    factor = inverse**3 * inner / L
    for i in range(12):
        cols = pl.ds(i * 128, 128)
        lat, cot, g = nat[:, cols], own[0:128, cols], gp_out[0:1, cols]
        gl_out[:, cols] = (inverse * g * cot - lat * factor).astype(BF16)
        nt_out[cols, :] = (lat * inverse * g).T.astype(BF16)
        gp_out[:, cols] = jnp.broadcast_to(jnp.sum(cot * lat * inverse, axis=0, keepdims=True), (8, 128))
    for copy in (
        sends
        + [n_copies[j, h] for j in range(3) for h in range(2)]
        + [q_copy, l_copy]
        + list(za.values()) + list(zb.values()) + list(yp.values()) + list(ym.values()) + list(yf.values())
    ):
        copy.wait_send()


def back(
    nt, gl, gp, ht, gq, gd_out, gu_out, gg_out,
    ntx, gx, g, hr, gla, gpa, xs, xr, zs, zr, us, ur, vs, vr,
    loc_sem, c_s, c_r, hs, hrs, gl_s, gl_r, gf_s, gf_r, gp_s, gp_r,
    z4_s, z4_r, na_s, na_r, nb_s, nb_r, d_s, d_r, e_s, e_r, u_s, u_r, v_s, v_r,
):
    x, y, z, c = coordinates()
    zh, zl = z // 4, lax.rem(z, 4)
    st = x * 2 + zh
    core_peer = device(x, y, z, c + 1)
    yc = [(dy, dc) for dy in (0, 1, 2, 3) for dc in (0, 1) if (dy, dc) != (0, 0)]
    meet(
        [device(x + d, y, z, c) for d in (1, 2, 3)]
        + [device(x, y, z + d, c) for d in range(1, 8)]
        + [device(x, y + dy, z, c + dc) for dy, dc in yc]
    )
    sends = []
    mine = y * 2 + c
    lanes_c = pl.ds(pl.multiple_of(c * 128, 128), 128)
    nt_core = send(nt.at[:, 1 - c], ntx.at[st, :, :, lanes_c], c_s.at[0], c_r.at[0], core_peer)
    nt_own = pltpu.make_async_copy(nt.at[:, c], ntx.at[st, :, :, lanes_c], loc_sem.at[0])
    nt_own.start()
    gl_copies = [
        send(gl, gla.at[mine], gl_s.at[i], gl_r.at[i], device(x, y + dy, z, c)) for i, dy in enumerate((2, 1, 3))
    ]
    gp_copies = [
        send(gp, gpa.at[mine], gp_s.at[i], gp_r.at[i], device(x, y + dy, z, c + dc))
        for i, (dy, dc) in enumerate(yc)
    ]
    gl_core = send(gl, gla.at[mine], gf_s.at[3], gf_r.at[3], core_peer)
    gl_own = pltpu.make_async_copy(gl, gla.at[mine], loc_sem.at[1])
    gl_own.start()
    gp_own = pltpu.make_async_copy(gp, gpa.at[mine], loc_sem.at[2])
    gp_own.start()
    nt_own.wait()
    nt_core.wait_recv()
    z4 = send(ntx.at[st], ntx.at[st], z4_s, z4_r, device(x, y, z + 4, c))
    na = [
        send(ntx.at[st], ntx.at[st], na_s.at[i], na_r.at[i], device(x + d, y, z, c))
        for i, d in enumerate((2, 1, 3))
    ]
    lanes_me = pl.ds(pl.multiple_of(mine * 128, 128), 128)
    h_copies = []
    for i, (dy, dc) in enumerate(yc):
        ty, tc = lax.rem(y + dy, 4), lax.rem(c + dc, 2)
        h_copies.append(
            send(ht.at[:, ty, tc], hr.at[:, :, lanes_me], hs.at[i], hrs.at[i], device(x, y + dy, z, c + dc))
        )
    h_own = pltpu.make_async_copy(ht.at[:, y, c], hr.at[:, :, lanes_me], loc_sem.at[3])
    h_own.start()
    gq_core = send(gq, gx.at[:, c], c_s.at[1], c_r.at[1], core_peer)
    gq_own = pltpu.make_async_copy(gq, gx.at[:, c], loc_sem.at[4])
    gq_own.start()
    sends += [nt_core, gl_core, z4, gq_core] + gl_copies + gp_copies + na + h_copies

    gl_fwd = []
    for i, dy in enumerate((2, 1, 3)):
        gl_copies[i].wait_recv()
        from_y = gla.at[lax.rem(y - dy + 4, 4) * 2 + c]
        gl_fwd.append(send(from_y, from_y, gf_s.at[i], gf_r.at[i], core_peer))
    sends += gl_fwd
    z4.wait_recv()
    other = ntx.at[st + 1 - 2 * zh]
    nb = [
        send(other, other, nb_s.at[i], nb_r.at[i], device(x + d, y, z, c)) for i, d in enumerate((2, 1, 3))
    ]
    sends += nb

    def product(zz, cols):
        value = None
        for i in range(4):
            slot = i * 2 + zz
            term = jnp.dot(
                ntx[slot].reshape(768, 256), gx[slot, :, :, cols].reshape(256, 256), preferred_element_type=F32
            )
            value = term if value is None else value + term
        return value

    gq_own.wait()
    gq_core.wait_recv()
    for copy in na:
        copy.wait_recv()

    def first(i, _):
        cols = pl.ds(pl.multiple_of(i * 256, 256), 256)
        g[:, cols] = product(zh, cols)
        return 0

    lax.fori_loop(0, 6, first, 0)

    gl_own.wait()
    gl_core.wait_recv()
    gp_own.wait()
    h_own.wait()
    for copy in gl_fwd + gp_copies + h_copies:
        copy.wait_recv()
    d_copies = []
    for j, d in enumerate((2, 1, 3, 0)):
        to = lax.rem(x + d, 4)
        cols = pl.ds(pl.multiple_of(to * 384, 128), 384)
        xs[j, 0:448, :] = jnp.dot(
            hr[...].reshape(448, 1024), gla[:, :, cols].reshape(1024, 384), preferred_element_type=F32
        )
        total = gpa[0, :, cols]
        for i in range(1, 8):
            total = total + gpa[i, :, cols]
        xs[j, 448:456, :] = total
        if d:
            d_copies.append(send(xs.at[j], xr.at[j], d_s.at[j], d_r.at[j], device(x + d, y, z, c)))
    sends += d_copies

    for copy in nb:
        copy.wait_recv()
    u_copies = {}
    for n in range(3):

        def second(i, _):
            cols = pl.ds(pl.multiple_of(n * 512 + i * 256, 256), 256)
            g[:, cols] = g[:, cols] + product(1 - zh, cols)
            return 0

        lax.fori_loop(0, 2, second, 0)
        cols = pl.ds(n * 512, 512)
        for j, d in enumerate((2, 1, 3)):
            ty = lax.rem(y + d, 4)
            for k in range(4):
                rows = pl.ds(pl.multiple_of((k * 4 + ty) * 48, 16), 48)
                us[n, j, k] = g[rows, cols].astype(BF16)
            u_copies[n, j] = send(us.at[n, j], ur.at[n, j], u_s.at[n, j], u_r.at[n, j], device(x, y + d, z, c))
    sends += list(u_copies.values())

    for copy in d_copies:
        copy.wait_recv()
    for a in range(2):
        for b in range(4):
            rows, cols = slice(b * 112, b * 112 + 112), slice(a * 192, a * 192 + 192)
            total, tail = xs[3, rows, cols], xs[3, 448:456, cols]
            for j in range(3):
                total = total + xr[j, rows, cols]
                tail = tail + xr[j, 448:456, cols]
            zs[a * 4 + b, 0:112, :] = total
            zs[a * 4 + b, 112:120, :] = tail
    e_copies = [
        send(zs.at[lax.rem(z + d, 8)], zr.at[d - 1], e_s.at[d - 1], e_r.at[d - 1], device(x, y, z + d, c))
        for d in (4, 3, 5, 2, 6, 1, 7)
    ]
    sends += e_copies

    v_copies = {}
    for n in range(3):
        cols = pl.ds(n * 512, 512)
        for j in range(3):
            u_copies[n, j].wait_recv()
        for k in range(4):
            rows = pl.ds(pl.multiple_of((k * 4 + y) * 48, 16), 48)
            total = g[rows, cols]
            for j in range(3):
                total = total + ur[n, j, k].astype(F32)
            g[rows, cols] = total
            vs[n, k] = total.astype(BF16)
        for d in (2, 1, 3):
            to = lax.rem(zl + d, 4)
            v_copies[n, d] = send(
                vs.at[n, to], vr.at[n, d - 1], v_s.at[n, d - 1], v_r.at[n, d - 1], device(x, y, zh * 4 + to, c)
            )
    sends += list(v_copies.values())

    for copy in e_copies:
        copy.wait_recv()
    total = zs[z]
    for j in range(7):
        total = total + zr[j]
    gd_out[...] = total[0:112]
    gg_out[...] = total[112:113]
    my_rows = pl.ds(pl.multiple_of((zl * 4 + y) * 48, 16), 48)
    for n in range(3):
        cols = pl.ds(n * 512, 512)
        for d in (1, 2, 3):
            v_copies[n, d].wait_recv()
        total = g[my_rows, cols]
        for j in range(3):
            total = total + vr[n, j].astype(F32)
        gu_out[:, cols] = total
    for copy in sends:
        copy.wait_send()


VMEM = pl.BlockSpec(memory_space=pltpu.VMEM)
ANY = pl.BlockSpec(memory_space=pl.ANY)


def dma(*shape):
    return pltpu.SemaphoreType.DMA(shape) if shape else pltpu.SemaphoreType.DMA


def pairs(*shapes):
    return [dma(*shape) for shape in shapes for _ in range(2)]


def run_front(hidden, w_down, norm_gain, w_up, grad_query):
    return pl.pallas_call(
        front,
        out_shape=(
            jax.ShapeDtypeStruct((1536, 128), BF16),
            jax.ShapeDtypeStruct((128, 1536), BF16),
            jax.ShapeDtypeStruct((8, 1536), F32),
            jax.ShapeDtypeStruct((3584, 128), BF16),
        ),
        in_specs=[VMEM, ANY, VMEM, VMEM, VMEM],
        out_specs=(VMEM, VMEM, VMEM, VMEM),
        scratch_shapes=[
            pltpu.VMEM((2, 128, 1792), BF16),
            pltpu.VMEM((4, SUB, 192), BF16),
            pltpu.VMEM((8, 1, 192), F32),
            pltpu.VMEM((2, 1792, 768), BF16),
            pltpu.VMEM((3, 256, 1536), BF16),
            pltpu.VMEM((3, 256, 1536), BF16),
            pltpu.VMEM((256, 1536), F32),
            pltpu.VMEM((128, 1536), F32),
            pltpu.VMEM((128, 1536), F32),
            pltpu.VMEM((2, 2, 128, 768), F32),
            pltpu.VMEM((2, 128, 768), F32),
            pltpu.VMEM((128, 1536), F32),
            dma(3),
        ]
        + pairs((3,), (7,), (), (3, 2), (), (4,), (3,), (8,), (8,), (8,), ()),
        compiler_params=pltpu.CompilerParams(
            collective_id=0, has_side_effects=True, vmem_limit_bytes=56 * 2**20
        ),
    )(hidden, w_down, norm_gain.reshape(1, 192), w_up, grad_query)


def run_back(normed, grad_latent, gain_part, hidden, grad_query):
    return pl.pallas_call(
        back,
        out_shape=(
            jax.ShapeDtypeStruct((112, 192), F32),
            jax.ShapeDtypeStruct((48, 1536), F32),
            jax.ShapeDtypeStruct((1, 192), F32),
        ),
        in_specs=[VMEM, VMEM, VMEM, VMEM, ANY],
        out_specs=(VMEM, VMEM, VMEM),
        scratch_shapes=[
            pltpu.VMEM((8, 16, 48, 256), BF16),
            pltpu.VMEM((8, 2, 128, 1536), BF16),
            pltpu.VMEM((768, 1536), F32),
            pltpu.VMEM((4, SUB, 1024), BF16),
            pltpu.VMEM((8, 128, 1536), BF16),
            pltpu.VMEM((8, 8, 1536), F32),
            pltpu.VMEM((4, 456, 384), F32),
            pltpu.VMEM((3, 456, 384), F32),
            pltpu.VMEM((8, 120, 192), F32),
            pltpu.VMEM((7, 120, 192), F32),
            pltpu.VMEM((3, 3, 4, 48, 512), BF16),
            pltpu.VMEM((3, 3, 4, 48, 512), BF16),
            pltpu.VMEM((3, 4, 48, 512), BF16),
            pltpu.VMEM((3, 3, 48, 512), BF16),
            dma(5),
        ]
        + pairs((2,), (7,), (3,), (4,), (7,), (), (3,), (3,), (3,), (7,), (3, 3), (3, 3)),
        compiler_params=pltpu.CompilerParams(
            collective_id=1, has_side_effects=True, vmem_limit_bytes=56 * 2**20
        ),
    )(
        normed.reshape(16, 2, 48, 128),
        grad_latent,
        gain_part,
        hidden.reshape(4, 4, 2, SUB, 128),
        grad_query.reshape(8, 128, 1536),
    )


def local(hidden, w_down, norm_gain, w_up, grad_query):
    normed, grad_latent, gain_part, turned = run_front(hidden, w_down, norm_gain, w_up, grad_query)
    grad_down, grad_up, grad_gain = run_back(normed, grad_latent, gain_part, turned, grad_query)
    return grad_down, grad_up, grad_gain.reshape(192)


def solution(mesh):
    placed = (P(("dp", "st"), None), P(None, "st"), P("st"), P(None, "st"), P("dp", "st"))
    return jax.shard_map(
        local,
        mesh=mesh,
        in_specs=placed,
        out_specs=(P("dp", "st"), P("dp", "st"), P("st")),
        check_vma=False,
    )
```

time: 729 us -> 199 us (0.27)
  waiting for transfers between devices: 558 us -> 0 us
  Pallas kernels: 0 us -> 190 us
  blocking collectives: 110 us -> 0 us
  matrix products: 32.4 us -> 0 us
  between operations: 13.8 us -> 0.65 us
    reduce_scatter x2 -> x0, waiting for transfers between devices: 282 us -> none  [the longest x1 157 us: local(): lax.psum_scatter(lax.dot_general(picked, grad_query, (((0,), (0,)), ((),...]
    all_gather x2 -> x0, waiting for transfers between devices: 210 us -> none  [the longest x1 152 us: local(): gathered = lax.all_gather(hidden, 'st', axis=0, tiled=True)]
    pallas_call x0 -> x2, Pallas kernels: none -> 190 us  [the longest x1 115 us: run_back(): pl.pallas_call(back, out_shape=(jax.ShapeDtypeStruct((112, 192), F32), ja...]
    psum x3 -> x0, blocking collectives: 110 us -> none  [the longest x1 68.4 us: local(): grad_gain = lax.psum(gain_part, 'dp')]
    unnamed x6 -> x0, waiting for transfers between devices: 65.6 us -> none
    dot_general x4 -> x0, matrix products: 32.4 us -> none  [the longest x1 9.36 us: local(): lax.dot_general(grad_query, w_up, (((1,), (1,)), ((), ())), preferred_ele...]
  transfers between devices with their start and end apart: 5 -> 0, of which waited for: 5 -> 0; matrix products, arithmetic and copies ran while one was open for 5% -> 0% of each run, Pallas kernels for 0% -> 0%
where the time goes in v1:
time: 199 us
  Pallas kernels  190 us (95%)
  local copies, waits for them, and re-layouts  8.19 us (4%)
    pallas_call x1, Pallas kernels, run_back(): pl.pallas_call(back, out_shape=(jax.ShapeDtypeStruct((112, 192), F32), ja...  115 us
    pallas_call x1, Pallas kernels, run_front(): pl.pallas_call(front, out_shape=(jax.ShapeDtypeStruct((1536, 128), BF16),...  75.6 us
    unnamed x4, local copies, waits for them, and re-layouts  8.19 us

profile of v1, /device:TPU:1, one launch (start us, length us, event | category | flops | bytes accessed | tf_op | source)
XLA Modules:
  0.0 199.2 jit_solution(7722902648392890438)
XLA Ops:
  0.6 3.6 %copy.8.wd = bf16[3584,192]{1,0:T(8,128)(2,1)} copy(bf16[3584,192]{0,1:T(8,128)(2,1)} %param.6) | data formatting | bytes 2752512 | tf_op args[1]
  4.3 75.6 %shard_map.76 = (bf16[1536,128]{1,0:T(8,128)(2,1)}, bf16[128,1536]{1,0:T(8,128)(2,1)}, f32[8,1536]{1,0:T(8,128)}, bf16[3584,128]{1,0:T(8,128)(2,1)}) custom-call(bf16[128,3584]{1,0:T(8,128)(2,1)} %hid.1, bf16[3584,192]{1,0:T(8,128)(2,1)} %copy.8.wd, f32[1,192]{1,0:T(1,128)} %bitcast.8, bf16[1536,1536]{1,0:T(8,128)(2,1)} %wup.1, bf16[1024,1536]{1,0:T(8,128)(2,1)} %gq.1), custom_call_target="tpu_custom_call" | custom-call | tf_op jit(solution)/shard_map/pallas_call | solution.py:449
  79.9 114.7 %shard_map.77 = (f32[112,192]{1,0:T(8,128)}, f32[48,1536]{1,0:T(8,128)}, f32[1,192]{1,0:T(1,128)}) custom-call(bf16[16,2,48,128]{3,2,1,0:T(8,128)(2,1)} %bitcast.7, bf16[128,1536]{1,0:T(8,128)(2,1)} %get-tuple-element.11.gl, f32[8,1536]{1,0:T(8,128)} %get-tuple-element.12.gp, bf16[4,4,2,112,128]{4,3,2,1,0:T(8,128)(2,1)} %bitcast.6, bf16[8,128,1536]{2,1,0:T(8,128)(2,1)} %bitcast.5), custom_call_target="tpu_custom_call" | custom-call | tf_op jit(solution)/shard_map/pallas_call | solution.py:482
  194.6 1.6 copy.9
  196.3 1.7 copy.12
  198.0 1.2 copy.13

commit v2 on v0

v2 whole, which is shorter than its diff:
```python
import functools

import jax
import jax.numpy as jnp
from jax import lax
from jax.experimental import pallas as pl
from jax.experimental.pallas import tpu as pltpu
from jax.sharding import PartitionSpec as P

L = 1536
MESH = pl.DeviceIdType.MESH
F32 = jnp.float32
BF16 = jnp.bfloat16
SUB = 112


def coordinates():
    dp = lax.axis_index("dp")
    st = lax.axis_index("st")
    zl, y, c = dp // 8, lax.rem(dp // 2, 4), lax.rem(dp, 2)
    x, zh = st // 2, lax.rem(st, 2)
    return x, y, zh * 4 + zl, c


def device(x, y, z, c):
    x, y, z, c = lax.rem(x + 8, 4), lax.rem(y + 8, 4), lax.rem(z + 16, 8), lax.rem(c + 2, 2)
    return ((lax.rem(z, 4) * 4 + y) * 2 + c, x * 2 + z // 4)


def send(src, dst, send_sem, recv_sem, to):
    copy = pltpu.make_async_remote_copy(
        src_ref=src, dst_ref=dst, send_sem=send_sem, recv_sem=recv_sem, device_id=to, device_id_type=MESH
    )
    copy.start()
    return copy


def whole(
    hid, wdt, gain, wup_hbm, gq, gd_out, gu_out, gg_out,
    wup, gx, wt, hk, xb, gb, w, snd, rcv, own, zs, zr, lp, lx, nat, ht,
    nt, nts, ntx, gla, gpa, hr, g, xs, xf, xo, xr, xfr, xg, xgr, ea, ear, eb, ebr, us, ur, vs, vr,
    loc_sem, x_s, x_r, g_s, g_r, h_s, h_r, n_s, n_r, q_s, q_r,
    za_s, za_r, zb_s, zb_r, yp_s, yp_r, ym_s, ym_r, yf_s, yf_r, l_s, l_r,
    c_s, c_r, t_s, t_r, glp_s, glp_r, glm_s, glm_r, glf_s, glf_r, glc_s, glc_r, gp_s, gp_r,
    z4_s, z4_r, np_s, np_r, nm_s, nm_r, nf_s, nf_r, d_s, d_r, dg_s, dg_r, e_s, e_r, u_s, u_r, v_s, v_r,
):
    x, y, z, c = coordinates()
    zh, zl = z // 4, lax.rem(z, 4)
    st = x * 2 + zh
    mine = y * 2 + c
    yc = [(dy, dc) for dy in (0, 1, 2, 3) for dc in (0, 1) if (dy, dc) != (0, 0)]
    s = 1 - 2 * c
    core_peer = device(x, y, z, c + 1)
    z4_peer = device(x, y, z + 4, c)
    up_x, down_x = device(x + 1, y, z, c), device(x - 1, y, z, c)
    up_y, down_y = device(x, y + 1, z, c), device(x, y - 1, z, c)
    up_z, down_z = device(x, y, z + s, c), device(x, y, z - s, c)
    peers = (
        [device(x + d, y, z, c) for d in (1, 2, 3)] + [up_y, down_y, up_z, down_z, z4_peer, core_peer]
    )
    barrier = pltpu.get_barrier_semaphore()
    for peer in peers:
        pl.semaphore_signal(barrier, inc=1, device_id=peer, device_id_type=MESH)
    loads = [
        pltpu.make_async_copy(gq, gx.at[:, c], loc_sem.at[0]),
        pltpu.make_async_copy(wup_hbm, wup, loc_sem.at[1]),
        pltpu.make_async_copy(hid.at[:, pl.ds(pl.multiple_of(c * 1792, 128), 1792)], hk.at[c], loc_sem.at[2]),
        pltpu.make_async_copy(gain, gb.at[zh, x], loc_sem.at[3]),
    ]
    for load in loads:
        load.start()
    row = (c * 16 + y * 4 + zl) * SUB
    base = jnp.minimum(row // 128, 26) * 128
    wt[...] = wdt[:, pl.ds(pl.multiple_of(base, 128), 256)].astype(F32).T.astype(BF16)
    piece = wt.at[pl.ds(pl.multiple_of(row - base, 16), SUB)]
    my_piece = pltpu.make_async_copy(piece, xb.at[x], loc_sem.at[4])
    my_piece.start()
    sends = []

    def cotangent(owner, store):
        def tile(i, _):
            cols = pl.ds(pl.multiple_of(i * 256, 256), 256)
            store(
                cols,
                lax.dot_general(
                    gx[pl.ds(owner * 2, 2), c].reshape(256, 1536),
                    wup[cols, :],
                    (((1,), (1,)), ((), ())),
                    preferred_element_type=F32,
                ),
            )
            return 0

        lax.fori_loop(0, 6, tile, 0)

    far = pl.ds(pl.multiple_of((1 - zh) * 128, 128), 128)
    near = pl.ds(pl.multiple_of(zh * 128, 128), 128)
    n_copies = {}

    def partial_for(j, d):
        def store(cols, value):
            snd[j, :, cols] = value.astype(BF16)

        cotangent(lax.rem(x + d, 4), store)

    def send_partial(j, d, h, rows):
        n_copies[j, h] = send(
            snd.at[j, rows], rcv.at[j, rows], n_s.at[j, h], n_r.at[j, h], device(x + d, y, z, c)
        )

    loads[0].wait()
    loads[1].wait()
    partial_for(0, 2)
    pl.semaphore_wait(barrier, len(peers))

    x_copies = [
        send(piece, xb.at[x], x_s.at[d - 1], x_r.at[d - 1], device(x + d, y, z, c)) for d in (2, 1, 3)
    ]
    send_partial(0, 2, 0, far)
    other_k = hid.at[:, pl.ds(pl.multiple_of((1 - c) * 1792, 128), 1792)]
    h_copy = send(other_k, hk.at[c], h_s, h_r, core_peer)
    g_copies = [
        send(gain, gb.at[zh, x], g_s.at[i], g_r.at[i], device(x + d, y, z, c)) for i, d in enumerate((2, 1, 3))
    ]
    gq_core = send(gq, gx.at[:, c], c_s.at[1], c_r.at[1], core_peer)
    sends += x_copies + [h_copy, gq_core] + g_copies

    partial_for(1, 1)
    send_partial(1, 1, 0, far)
    my_piece.wait()
    for copy in x_copies:
        copy.wait_recv()
    loads[3].wait()
    for copy in g_copies:
        copy.wait_recv()
    g_across = send(gb.at[zh], gb.at[zh], g_s.at[3], g_r.at[3], z4_peer)
    sends += [g_across]

    def unit(zz, yy):
        zz, yy = lax.rem(zz + 16, 8), lax.rem(yy + 8, 4)
        rows = pl.multiple_of((yy * 4 + lax.rem(zz, 4)) * SUB, 16)
        return w.at[zz // 4, pl.ds(rows, SUB)]

    my_rows = pl.ds(pl.multiple_of((y * 4 + zl) * SUB, 16), SUB)
    for i in range(4):
        w[zh, my_rows, i * 192 : (i + 1) * 192] = xb[i]

    owners = [z, z - s, z + s, z - 2 * s, z + 2 * s, z - 3 * s, z + 3 * s, z - 4 * s]
    za, zb, yp, ym, yf = {}, {}, {}, {}, {}

    def pass_on(k):
        here = unit(owners[k], y)
        if k == 0 or (k % 2 == 1 and k < 7):
            i = (k + 1) // 2
            za[i] = send(here, here, za_s.at[i], za_r.at[i], up_z)
        if k == 0 or (k % 2 == 0 and k < 6):
            i = k // 2
            zb[i] = send(here, here, zb_s.at[i], zb_r.at[i], down_z)
        yp[k] = send(here, here, yp_s.at[k], yp_r.at[k], up_y)
        ym[k] = send(here, here, ym_s.at[k], ym_r.at[k], down_y)

    def forward(k):
        yp[k].wait_recv()
        ym[k].wait_recv()
        if k % 2 == 0:
            there = unit(owners[k], y - 1)
            yf[k] = send(there, there, yf_s.at[k], yf_r.at[k], up_y)
        else:
            there = unit(owners[k], y + 1)
            yf[k] = send(there, there, yf_s.at[k], yf_r.at[k], down_y)

    pass_on(0)
    partial_for(2, 3)
    send_partial(2, 3, 0, far)
    def keep(cols, value):
        own[:, cols] = value

    za[0].wait_recv()
    pass_on(1)
    zb[0].wait_recv()
    pass_on(2)
    cotangent(x, keep)
    forward(0)
    for j, d in enumerate((2, 1, 3)):
        n_copies[j, 0].wait_send()
        send_partial(j, d, 1, near)
    za[1].wait_recv()
    pass_on(3)
    zb[1].wait_recv()
    pass_on(4)

    def turn(i, _):
        cols = pl.ds(pl.multiple_of(i * 896, 128), 896)
        ht[i] = hid[:, cols].astype(F32).T.astype(BF16).reshape(4, 2, SUB, 128)
        return 0

    forward(1)
    for j in range(3):
        n_copies[j, 0].wait_recv()
    total = own[far, :]
    for j in range(3):
        total = total + rcv[j, far, :].astype(F32)
    zs[...] = total.astype(BF16)
    q_copy = send(zs, zr, q_s, q_r, z4_peer)
    za[2].wait_recv()
    pass_on(5)
    zb[2].wait_recv()
    pass_on(6)
    forward(2)
    lax.fori_loop(0, 4, turn, 0)
    forward(3)
    za[3].wait_recv()
    pass_on(7)
    forward(4)
    forward(5)
    forward(6)
    forward(7)
    lanes_me = pl.ds(pl.multiple_of(mine * 128, 128), 128)
    t_copies = []
    for i, (dy, dc) in enumerate(yc):
        ty, tc = lax.rem(y + dy, 4), lax.rem(c + dc, 2)
        t_copies.append(
            send(ht.at[:, ty, tc], hr.at[:, :, lanes_me], t_s.at[i], t_r.at[i], device(x, y + dy, z, c + dc))
        )
    t_own = pltpu.make_async_copy(ht.at[:, y, c], hr.at[:, :, lanes_me], loc_sem.at[5])
    t_own.start()
    sends += t_copies
    for k in range(8):
        yf[k].wait_recv()
    h_copy.wait_recv()
    loads[2].wait()

    for half in range(2):

        def tile(i, _):
            cols = pl.ds(pl.multiple_of(i * 256, 256), 256)
            value = jnp.dot(hk[...].reshape(256, 1792), w[half, :, cols], preferred_element_type=F32)
            lp[:, half, :, cols] = value.reshape(2, 128, 256)
            return 0

        lax.fori_loop(0, 3, tile, 0)
    l_copy = send(lp.at[1 - c], lx, l_s, l_r, core_peer)

    g_across.wait_recv()
    for j in range(3):
        n_copies[j, 1].wait_recv()
    q_copy.wait_recv()
    total = own[near, :] + zr[...].astype(F32)
    for j in range(3):
        total = total + rcv[j, near, :].astype(F32)
    own[0:128, :] = total
    for i in range(8):
        gpa[mine, :, i * 192 : (i + 1) * 192] = gb[i % 2, i // 2]
    l_copy.wait_recv()
    for half in range(2):
        for i in range(4):
            piece_cols = pl.ds(i * 192, 192)
            at = i * 384 + half * 192
            nat[:, at : at + 192] = lp[c, half, :, piece_cols] + lx[half, :, piece_cols]
    latent = nat[...]
    inverse = lax.rsqrt(jnp.sum(latent * latent, axis=1, keepdims=True) / L + 1e-06)
    for i in range(12):
        cols = pl.ds(i * 128, 128)
        nt[cols, :] = (nat[:, cols] * inverse * gpa[mine, :, cols]).T.astype(BF16)
    lanes_c = pl.ds(pl.multiple_of(c * 128, 128), 128)
    for i in range(16):
        nts[i] = nt[pl.ds(pl.multiple_of(i * 96 + (1 - c) * 48, 16), 48), :]
    nt_core = send(nts, ntx.at[st, :, :, lanes_c], c_s.at[0], c_r.at[0], core_peer)
    for i in range(16):
        ntx[st, i, :, lanes_c] = nt[pl.ds(pl.multiple_of(i * 96 + c * 48, 16), 48), :]
    inner = jnp.sum(gpa[mine] * own[0:128, :] * nat[...], axis=1, keepdims=True)
    factor = inverse**3 * inner / L
    for i in range(12):
        cols = pl.ds(i * 128, 128)
        lat, cot = nat[:, cols], own[0:128, cols]
        value = inverse * gpa[mine, :, cols] * cot - lat * factor
        high = value.astype(BF16)
        gla[0, mine, :, cols] = high
        gla[1, mine, :, cols] = (value - high.astype(F32)).astype(BF16)
        gpa[mine, :, cols] = jnp.sum(cot * lat * inverse, axis=0, keepdims=True)

    mine_gl = [gla.at[v, mine] for v in range(2)]
    nt_core.wait_recv()
    glp = [send(mine_gl[0], mine_gl[0], glp_s.at[0], glp_r.at[0], up_y)]
    glm = [send(mine_gl[0], mine_gl[0], glm_s.at[0], glm_r.at[0], down_y)]

    def part(slot, h):
        return ntx.at[slot, pl.ds(h * 8, 8)]

    z4 = [send(part(st, h), part(st, h), z4_s.at[h], z4_r.at[h], z4_peer) for h in range(2)]
    np_, nm, nf = {}, {}, {}

    def spread(a, slot, order):
        for up, h in order:
            there = part(slot, h)
            if up:
                np_[a, h] = send(there, there, np_s.at[a, h], np_r.at[a, h], up_x)
            else:
                nm[a, h] = send(there, there, nm_s.at[a, h], nm_r.at[a, h], down_x)

    def relay(a, side):
        np_[a, 0].wait_recv()
        there = part(lax.rem(x + 3, 4) * 2 + side, 0)
        nf[a, 0] = send(there, there, nf_s.at[a, 0], nf_r.at[a, 0], up_x)
        nm[a, 1].wait_recv()
        there = part(lax.rem(x + 1, 4) * 2 + side, 1)
        nf[a, 1] = send(there, there, nf_s.at[a, 1], nf_r.at[a, 1], down_x)

    spread(0, st, ((True, 0), (False, 1), (False, 0), (True, 1)))
    glp.append(send(mine_gl[1], mine_gl[1], glp_s.at[1], glp_r.at[1], up_y))
    glm.append(send(mine_gl[1], mine_gl[1], glm_s.at[1], glm_r.at[1], down_y))
    gp_copies = [
        send(gpa.at[mine], gpa.at[mine], gp_s.at[i], gp_r.at[i], device(x, y + dy, z, c + dc))
        for i, (dy, dc) in enumerate(yc)
    ]
    glc = [send(mine_gl[v], mine_gl[v], glc_s.at[0, v], glc_r.at[0, v], core_peer) for v in range(2)]
    relay(0, zh)

    def to_core(v, i, dy):
        slot = gla.at[v, lax.rem(y + dy, 4) * 2 + c]
        glc.append(send(slot, slot, glc_s.at[i, v], glc_r.at[i, v], core_peer))
        return slot

    glp[0].wait_recv()
    slot = to_core(0, 1, 3)
    glf = [send(slot, slot, glf_s.at[0], glf_r.at[0], up_y)]
    glm[0].wait_recv()
    to_core(0, 2, 1)
    side = 1 - zh
    other = x * 2 + side
    z4[0].wait_recv()
    spread(1, other, ((True, 0), (False, 0)))

    def product(zz, cols):
        value = None
        for i in range(4):
            slot = i * 2 + zz
            term = jnp.dot(
                ntx[slot].reshape(768, 256), gx[slot, :, :, cols].reshape(256, 256), preferred_element_type=F32
            )
            value = term if value is None else value + term
        return value

    gq_core.wait_recv()
    np_[0, 1].wait_recv()
    nm[0, 0].wait_recv()
    nf[0, 0].wait_recv()
    nf[0, 1].wait_recv()

    def first(i, _):
        cols = pl.ds(pl.multiple_of(i * 256, 256), 256)
        g[:, cols] = product(zh, cols)
        return 0

    lax.fori_loop(0, 3, first, 0)
    z4[1].wait_recv()
    spread(1, other, ((False, 1), (True, 1)))
    glm[1].wait_recv()
    slot = to_core(1, 2, 1)
    glf.append(send(slot, slot, glf_s.at[1], glf_r.at[1], down_y))
    glp[1].wait_recv()
    to_core(1, 1, 3)
    lax.fori_loop(3, 6, first, 0)
    relay(1, side)
    glf[0].wait_recv()
    to_core(0, 3, 2)
    glf[1].wait_recv()
    to_core(1, 3, 2)
    sends += z4 + glp + glm + glf + glc + gp_copies + [nt_core]

    np_[1, 1].wait_recv()
    nm[1, 0].wait_recv()
    nf[1, 0].wait_recv()
    nf[1, 1].wait_recv()
    sends += list(np_.values()) + list(nm.values()) + list(nf.values())
    u_copies = {}
    for n in range(3):

        def second(i, _):
            cols = pl.ds(pl.multiple_of(n * 512 + i * 256, 256), 256)
            g[:, cols] = g[:, cols] + product(1 - zh, cols)
            return 0

        lax.fori_loop(0, 2, second, 0)
        cols = pl.ds(n * 512, 512)
        for j, d in enumerate((2, 1, 3)):
            ty = lax.rem(y + d, 4)
            for k in range(4):
                rows = pl.ds(pl.multiple_of((k * 4 + ty) * 48, 16), 48)
                us[n, j, k] = g[rows, cols].astype(BF16)
            u_copies[n, j] = send(us.at[n, j], ur.at[n, j], u_s.at[n, j], u_r.at[n, j], device(x, y + d, z, c))
    sends += list(u_copies.values())

    t_own.wait()
    for copy in glc + gp_copies + t_copies:
        copy.wait_recv()
    d_copies, dg_copies = {}, []
    split = (pl.ds(0, 64), pl.ds(64, 48))

    def outgoing(j):
        return xs if j == 0 else xf.at[j - 1]

    def arrived(j):
        return xr if j == 0 else xfr.at[j - 1]

    def send_down(j, d, h):
        d_copies[j, h] = send(
            outgoing(j).at[:, split[h]], arrived(j).at[:, split[h]],
            d_s.at[j, h], d_r.at[j, h], device(x + d, y, z, c),
        )

    for j, d in enumerate((2, 1, 3, 0)):
        to = lax.rem(x + d, 4)
        cols = pl.ds(pl.multiple_of(to * 384, 128), 384)
        rows = hr[...].reshape(448, 1024)
        value = jnp.dot(rows, gla[0, :, :, cols].reshape(1024, 384), preferred_element_type=F32) + jnp.dot(
            rows, gla[1, :, :, cols].reshape(1024, 384), preferred_element_type=F32
        )
        value = value.reshape(4, SUB, 384)
        total = gpa[0, :, cols]
        for i in range(1, 8):
            total = total + gpa[i, :, cols]
        xg[j] = jnp.broadcast_to(total, (8, 384))
        if d:
            outgoing(j)[...] = value.astype(outgoing(j).dtype)
            send_down(j, d, 0)
            dg_copies.append(send(xg.at[j], xgr.at[j], dg_s.at[j], dg_r.at[j], device(x + d, y, z, c)))
        else:
            xo[...] = value
    for j, d in enumerate((2, 1, 3)):
        send_down(j, d, 1)
    sends += list(d_copies.values()) + dg_copies

    v_copies = {}

    def narrow(n):
        cols = pl.ds(n * 512, 512)
        for j in range(3):
            u_copies[n, j].wait_recv()
        for k in range(4):
            rows = pl.ds(pl.multiple_of((k * 4 + y) * 48, 16), 48)
            total = g[rows, cols]
            for j in range(3):
                total = total + ur[n, j, k].astype(F32)
            g[rows, cols] = total
            vs[n, k] = total.astype(BF16)
        for d in (2, 1, 3):
            to = lax.rem(zl + d, 4)
            v_copies[n, d] = send(
                vs.at[n, to], vr.at[n, d - 1], v_s.at[n, d - 1], v_r.at[n, d - 1], device(x, y, zh * 4 + to, c)
            )

    e_copies = {}

    def deliver(h, buffer, landing):
        begin, size = ((0, 64), (64, 48))[h]
        for j in range(3):
            d_copies[j, h].wait_recv()
        for b in range(4):
            total = xo[b, begin : begin + size, :]
            for j in range(3):
                total = total + arrived(j)[b, begin : begin + size, :].astype(F32)
            xo[b, begin : begin + size, :] = total
            for a in range(2):
                at, mid = a * 192, begin + size // 2
                i = a * 4 + b
                buffer[i, 0:size, :] = xo[b, begin : begin + size, at : at + 128]
                buffer[i, size : size + size // 2, 0:64] = xo[b, begin:mid, at + 128 : at + 192]
                buffer[i, size : size + size // 2, 64:128] = xo[b, mid : begin + size, at + 128 : at + 192]
        if h:
            for copy in dg_copies:
                copy.wait_recv()
            total = xg[3]
            for j in range(3):
                total = total + xgr[j]
            xg[3] = total
            for a in range(2):
                for b in range(4):
                    buffer[a * 4 + b, 72:80, :] = jnp.zeros((8, 128), F32)
                    buffer[a * 4 + b, 72:73, :] = xg[3, 0:1, a * 192 : a * 192 + 128]
                    buffer[a * 4 + b, 73:74, 0:64] = xg[3, 0:1, a * 192 + 128 : a * 192 + 192]
        for d in (4, 3, 5, 2, 6, 1, 7):
            e_copies[h, d] = send(
                buffer.at[lax.rem(z + d, 8)], landing.at[d - 1],
                e_s.at[h, d - 1], e_r.at[h, d - 1], device(x, y, z + d, c),
            )

    narrow(0)
    deliver(0, ea, ear)
    narrow(1)
    deliver(1, eb, ebr)
    narrow(2)
    sends += list(v_copies.values()) + list(e_copies.values())

    for h, (buffer, landing) in enumerate(((ea, ear), (eb, ebr))):
        begin, size = ((0, 64), (64, 48))[h]
        for d in range(1, 8):
            e_copies[h, d].wait_recv()
        total = buffer[z]
        for j in range(7):
            total = total + landing[j]
        half = size // 2
        gd_out[begin : begin + size, 0:128] = total[0:size]
        gd_out[begin : begin + half, 128:192] = total[size : size + half, 0:64]
        gd_out[begin + half : begin + size, 128:192] = total[size : size + half, 64:128]
        if h:
            gg_out[:, 0:128] = total[72:73]
            gg_out[:, 128:192] = total[73:74, 0:64]
    my_rows = pl.ds(pl.multiple_of((zl * 4 + y) * 48, 16), 48)
    for n in range(3):
        cols = pl.ds(n * 512, 512)
        for d in (1, 2, 3):
            v_copies[n, d].wait_recv()
        total = g[my_rows, cols]
        for j in range(3):
            total = total + vr[n, j].astype(F32)
        gu_out[:, cols] = total
    sends += [n_copies[j, 1] for j in range(3)] + [q_copy, l_copy]
    for group in (za, zb, yp, ym, yf):
        sends += list(group.values())
    for copy in sends:
        copy.wait_send()


VMEM = pl.BlockSpec(memory_space=pltpu.VMEM)
ANY = pl.BlockSpec(memory_space=pl.ANY)


def dma(*shape):
    return pltpu.SemaphoreType.DMA(shape) if shape else pltpu.SemaphoreType.DMA


def pairs(*shapes):
    return [dma(*shape) for shape in shapes for _ in range(2)]


def local(hidden, w_down, norm_gain, w_up, grad_query):
    grad_down, grad_up, grad_gain = pl.pallas_call(
        whole,
        out_shape=(
            jax.ShapeDtypeStruct((112, 192), F32),
            jax.ShapeDtypeStruct((48, 1536), F32),
            jax.ShapeDtypeStruct((1, 192), F32),
        ),
        in_specs=[VMEM, VMEM, VMEM, ANY, ANY],
        out_specs=(VMEM, VMEM, VMEM),
        scratch_shapes=[
            pltpu.VMEM((1536, 1536), BF16),
            pltpu.VMEM((8, 2, 128, 1536), BF16),
            pltpu.VMEM((256, 192), BF16),
            pltpu.VMEM((2, 128, 1792), BF16),
            pltpu.VMEM((4, SUB, 192), BF16),
            pltpu.VMEM((2, 4, 1, 192), F32),
            pltpu.VMEM((2, 1792, 768), BF16),
            pltpu.VMEM((3, 256, 1536), BF16),
            pltpu.VMEM((3, 256, 1536), BF16),
            pltpu.VMEM((256, 1536), F32),
            pltpu.VMEM((128, 1536), BF16),
            pltpu.VMEM((128, 1536), BF16),
            pltpu.VMEM((2, 2, 128, 768), F32),
            pltpu.VMEM((2, 128, 768), F32),
            pltpu.VMEM((128, 1536), F32),
            pltpu.VMEM((4, 4, 2, SUB, 128), BF16),
            pltpu.VMEM((1536, 128), BF16),
            pltpu.VMEM((16, 48, 128), BF16),
            pltpu.VMEM((8, 16, 48, 256), BF16),
            pltpu.VMEM((2, 8, 128, 1536), BF16),
            pltpu.VMEM((8, 1, 1536), F32),
            pltpu.VMEM((4, SUB, 1024), BF16),
            pltpu.VMEM((768, 1536), F32),
            pltpu.VMEM((4, SUB, 384), BF16),
            pltpu.VMEM((2, 4, SUB, 384), F32),
            pltpu.VMEM((4, SUB, 384), F32),
            pltpu.VMEM((4, SUB, 384), BF16),
            pltpu.VMEM((2, 4, SUB, 384), F32),
            pltpu.VMEM((4, 8, 384), F32),
            pltpu.VMEM((3, 8, 384), F32),
            pltpu.VMEM((8, 96, 128), F32),
            pltpu.VMEM((7, 96, 128), F32),
            pltpu.VMEM((8, 80, 128), F32),
            pltpu.VMEM((7, 80, 128), F32),
            pltpu.VMEM((3, 3, 4, 48, 512), BF16),
            pltpu.VMEM((3, 3, 4, 48, 512), BF16),
            pltpu.VMEM((3, 4, 48, 512), BF16),
            pltpu.VMEM((3, 3, 48, 512), BF16),
            dma(6),
        ]
        + pairs((3,), (4,), (), (3, 2), (), (4,), (3,), (8,), (8,), (8,), ())
        + pairs((2,), (7,), (2,), (2,), (2,), (4, 2), (7,), (2,), (2, 2), (2, 2), (2, 2), (3, 2), (3,), (2, 7))
        + pairs((3, 3), (3, 3)),
        compiler_params=pltpu.CompilerParams(
            collective_id=0, has_side_effects=True, vmem_limit_bytes=62 * 2**20
        ),
    )(hidden, w_down.T, norm_gain.reshape(1, 192), w_up, grad_query.reshape(8, 128, 1536))
    return grad_down, grad_up, grad_gain.reshape(192)


def solution(mesh):
    placed = (P(("dp", "st"), None), P(None, "st"), P("st"), P(None, "st"), P("dp", "st"))
    return jax.shard_map(
        local,
        mesh=mesh,
        in_specs=placed,
        out_specs=(P("dp", "st"), P("dp", "st"), P("st")),
        check_vma=False,
    )
```

time: 729 us -> 171 us (0.23)
  waiting for transfers between devices: 558 us -> 0 us
  Pallas kernels: 0 us -> 164 us
  blocking collectives: 110 us -> 0 us
  matrix products: 32.4 us -> 0 us
  between operations: 13.8 us -> 0.64 us
    reduce_scatter x2 -> x0, waiting for transfers between devices: 282 us -> none  [the longest x1 157 us: local(): lax.psum_scatter(lax.dot_general(picked, grad_query, (((0,), (0,)), ((),...]
    all_gather x2 -> x0, waiting for transfers between devices: 210 us -> none  [the longest x1 152 us: local(): gathered = lax.all_gather(hidden, 'st', axis=0, tiled=True)]
    pallas_call x0 -> x1, Pallas kernels: none -> 164 us  [local(): pl.pallas_call(whole, out_shape=(jax.ShapeDtypeStruct((112, 192), F32), j...]
    psum x3 -> x0, blocking collectives: 110 us -> none  [the longest x1 68.4 us: local(): grad_gain = lax.psum(gain_part, 'dp')]
    unnamed x6 -> x0, waiting for transfers between devices: 65.6 us -> none
    dot_general x4 -> x0, matrix products: 32.4 us -> none  [the longest x1 9.36 us: local(): lax.dot_general(grad_query, w_up, (((1,), (1,)), ((), ())), preferred_ele...]
  transfers between devices with their start and end apart: 5 -> 0, of which waited for: 5 -> 0; matrix products, arithmetic and copies ran while one was open for 5% -> 0% of each run, Pallas kernels for 0% -> 0%
where the time goes in v2:
time: 171 us; the launch traced here: 169 us
  Pallas kernels  164 us (96%)
  local copies, waits for them, and re-layouts  4.58 us (3%)
    pallas_call x1, Pallas kernels, local(): pl.pallas_call(whole, out_shape=(jax.ShapeDtypeStruct((112, 192), F32), j...  164 us
    unnamed x3, local copies, waits for them, and re-layouts  4.58 us

profile of v2, /device:TPU:1, one launch (start us, length us, event | category | flops | bytes accessed | tf_op | source)
XLA Modules:
  0.0 169.2 jit_solution(5815592866182771762)
XLA Ops:
  0.6 164.0 %shard_map.76 = (f32[112,192]{1,0:T(8,128)}, f32[48,1536]{1,0:T(8,128)}, f32[1,192]{1,0:T(1,128)}) custom-call(bf16[128,3584]{1,0:T(8,128)(2,1)} %hid.1, bf16[192,3584]{1,0:T(8,128)(2,1)} %bitcast.5, f32[1,192]{1,0:T(1,128)} %bitcast.7, bf16[1536,1536]{1,0:T(8,128)(2,1)} %wup_hbm.1, bf16[8,128,1536]{2,1,0:T(8,128)(2,1)} %bitcast.4), custom_call_target="tpu_custom_call" | custom-call | tf_op jit(solution)/shard_map/pallas_call | solution.py:538
  164.6 1.6 copy.8
  166.3 1.7 %copy.11 = f32[48,1536]{1,0:T(8,128)} copy(f32[48,1536]{1,0:T(8,128)} %get-tuple-element.16) | data formatting | bytes 589824
  168.0 1.2 copy.12

commit v3 on v2

--- a/solution.py
+++ b/solution.py
@@ -12,6 +12,7 @@
 F32 = jnp.float32
 BF16 = jnp.bfloat16
 SUB = 112
+PARTS = ((0, 48), (48, 48), (96, 16))
 
 
 def coordinates():
@@ -37,8 +38,8 @@
 
 def whole(
     hid, wdt, gain, wup_hbm, gq, gd_out, gu_out, gg_out,
-    wup, gx, wt, hk, xb, gb, w, snd, rcv, own, zs, zr, lp, lx, nat, ht,
-    nt, nts, ntx, gla, gpa, hr, g, xs, xf, xo, xr, xfr, xg, xgr, ea, ear, eb, ebr, us, ur, vs, vr,
+    hidv, wdv, wup, gx, wt, hk, xb, gb, w, snd, rcv, own, zs, zr, lp, lx, nat, ht,
+    nt, nts, ntx, gla, gpa, hr, g, xs, xf, xo, xr, xfr, xg, xgr, ea, ear, eb, ebr, ec, ecr, us, ur, vs, vr,
     loc_sem, x_s, x_r, g_s, g_r, h_s, h_r, n_s, n_r, q_s, q_r,
     za_s, za_r, zb_s, zb_r, yp_s, yp_r, ym_s, ym_r, yf_s, yf_r, l_s, l_r,
     c_s, c_r, t_s, t_r, glp_s, glp_r, glm_s, glm_r, glf_s, glf_r, glc_s, glc_r, gp_s, gp_r,
@@ -66,12 +67,17 @@
         pltpu.make_async_copy(wup_hbm, wup, loc_sem.at[1]),
         pltpu.make_async_copy(hid.at[:, pl.ds(pl.multiple_of(c * 1792, 128), 1792)], hk.at[c], loc_sem.at[2]),
         pltpu.make_async_copy(gain, gb.at[zh, x], loc_sem.at[3]),
+        pltpu.make_async_copy(hid, hidv, loc_sem.at[6]),
     ]
-    for load in loads:
-        load.start()
     row = (c * 16 + y * 4 + zl) * SUB
     base = jnp.minimum(row // 128, 26) * 128
-    wt[...] = wdt[:, pl.ds(pl.multiple_of(base, 128), 256)].astype(F32).T.astype(BF16)
+    window = pltpu.make_async_copy(wdt.at[:, pl.ds(pl.multiple_of(base, 128), 256)], wdv, loc_sem.at[7])
+    window.start()
+    loads[4].start()
+    for load in loads[:4]:
+        load.start()
+    window.wait()
+    wt[...] = wdv[...].astype(F32).T.astype(BF16)
     piece = wt.at[pl.ds(pl.multiple_of(row - base, 16), SUB)]
     my_piece = pltpu.make_async_copy(piece, xb.at[x], loc_sem.at[4])
     my_piece.start()
@@ -103,20 +109,30 @@
 
         cotangent(lax.rem(x + d, 4), store)
 
+    def keep(cols, value):
+        own[:, cols] = value
+
     def send_partial(j, d, h, rows):
         n_copies[j, h] = send(
             snd.at[j, rows], rcv.at[j, rows], n_s.at[j, h], n_r.at[j, h], device(x + d, y, z, c)
         )
 
+    def turn(i, _):
+        cols = pl.ds(pl.multiple_of(i * 896, 128), 896)
+        ht[i] = hidv[:, cols].astype(F32).T.astype(BF16).reshape(4, 2, SUB, 128)
+        return 0
+
+    loads[4].wait()
+    lax.fori_loop(0, 4, turn, 0)
     loads[0].wait()
     loads[1].wait()
     partial_for(0, 2)
+    partial_for(1, 1)
     pl.semaphore_wait(barrier, len(peers))
 
     x_copies = [
         send(piece, xb.at[x], x_s.at[d - 1], x_r.at[d - 1], device(x + d, y, z, c)) for d in (2, 1, 3)
     ]
-    send_partial(0, 2, 0, far)
     other_k = hid.at[:, pl.ds(pl.multiple_of((1 - c) * 1792, 128), 1792)]
     h_copy = send(other_k, hk.at[c], h_s, h_r, core_peer)
     g_copies = [
@@ -125,8 +141,7 @@
     gq_core = send(gq, gx.at[:, c], c_s.at[1], c_r.at[1], core_peer)
     sends += x_copies + [h_copy, gq_core] + g_copies
 
-    partial_for(1, 1)
-    send_partial(1, 1, 0, far)
+    partial_for(2, 3)
     my_piece.wait()
     for copy in x_copies:
         copy.wait_recv()
@@ -170,31 +185,28 @@
             yf[k] = send(there, there, yf_s.at[k], yf_r.at[k], down_y)
 
     pass_on(0)
-    partial_for(2, 3)
-    send_partial(2, 3, 0, far)
-    def keep(cols, value):
-        own[:, cols] = value
-
+    for j, d in enumerate((2, 1, 3)):
+        send_partial(j, d, 0, far)
+    cotangent(x, keep)
     za[0].wait_recv()
     pass_on(1)
     zb[0].wait_recv()
     pass_on(2)
-    cotangent(x, keep)
     forward(0)
-    for j, d in enumerate((2, 1, 3)):
-        n_copies[j, 0].wait_send()
-        send_partial(j, d, 1, near)
     za[1].wait_recv()
     pass_on(3)
     zb[1].wait_recv()
     pass_on(4)
 
-    def turn(i, _):
-        cols = pl.ds(pl.multiple_of(i * 896, 128), 896)
-        ht[i] = hid[:, cols].astype(F32).T.astype(BF16).reshape(4, 2, SUB, 128)
-        return 0
-
     forward(1)
+    for j, d in enumerate((2, 1, 3)):
+        n_copies[j, 0].wait_send()
+        send_partial(j, d, 1, near)
+    za[2].wait_recv()
+    pass_on(5)
+    zb[2].wait_recv()
+    pass_on(6)
+    forward(2)
     for j in range(3):
         n_copies[j, 0].wait_recv()
     total = own[far, :]
@@ -202,12 +214,6 @@
         total = total + rcv[j, far, :].astype(F32)
     zs[...] = total.astype(BF16)
     q_copy = send(zs, zr, q_s, q_r, z4_peer)
-    za[2].wait_recv()
-    pass_on(5)
-    zb[2].wait_recv()
-    pass_on(6)
-    forward(2)
-    lax.fori_loop(0, 4, turn, 0)
     forward(3)
     za[3].wait_recv()
     pass_on(7)
@@ -280,13 +286,13 @@
         gpa[mine, :, cols] = jnp.sum(cot * lat * inverse, axis=0, keepdims=True)
 
     mine_gl = [gla.at[v, mine] for v in range(2)]
-    nt_core.wait_recv()
     glp = [send(mine_gl[0], mine_gl[0], glp_s.at[0], glp_r.at[0], up_y)]
     glm = [send(mine_gl[0], mine_gl[0], glm_s.at[0], glm_r.at[0], down_y)]
 
     def part(slot, h):
         return ntx.at[slot, pl.ds(h * 8, 8)]
 
+    nt_core.wait_recv()
     z4 = [send(part(st, h), part(st, h), z4_s.at[h], z4_r.at[h], z4_peer) for h in range(2)]
     np_, nm, nf = {}, {}, {}
 
@@ -368,34 +374,11 @@
     to_core(1, 3, 2)
     sends += z4 + glp + glm + glf + glc + gp_copies + [nt_core]
 
-    np_[1, 1].wait_recv()
-    nm[1, 0].wait_recv()
-    nf[1, 0].wait_recv()
-    nf[1, 1].wait_recv()
-    sends += list(np_.values()) + list(nm.values()) + list(nf.values())
-    u_copies = {}
-    for n in range(3):
-
-        def second(i, _):
-            cols = pl.ds(pl.multiple_of(n * 512 + i * 256, 256), 256)
-            g[:, cols] = g[:, cols] + product(1 - zh, cols)
-            return 0
-
-        lax.fori_loop(0, 2, second, 0)
-        cols = pl.ds(n * 512, 512)
-        for j, d in enumerate((2, 1, 3)):
-            ty = lax.rem(y + d, 4)
-            for k in range(4):
-                rows = pl.ds(pl.multiple_of((k * 4 + ty) * 48, 16), 48)
-                us[n, j, k] = g[rows, cols].astype(BF16)
-            u_copies[n, j] = send(us.at[n, j], ur.at[n, j], u_s.at[n, j], u_r.at[n, j], device(x, y + d, z, c))
-    sends += list(u_copies.values())
-
     t_own.wait()
     for copy in glc + gp_copies + t_copies:
         copy.wait_recv()
     d_copies, dg_copies = {}, []
-    split = (pl.ds(0, 64), pl.ds(64, 48))
+    split = [pl.ds(begin, size) for begin, size in PARTS]
 
     def outgoing(j):
         return xs if j == 0 else xf.at[j - 1]
@@ -427,9 +410,33 @@
             dg_copies.append(send(xg.at[j], xgr.at[j], dg_s.at[j], dg_r.at[j], device(x + d, y, z, c)))
         else:
             xo[...] = value
-    for j, d in enumerate((2, 1, 3)):
-        send_down(j, d, 1)
+    for h in (1, 2):
+        for j, d in enumerate((2, 1, 3)):
+            send_down(j, d, h)
     sends += list(d_copies.values()) + dg_copies
+
+    np_[1, 1].wait_recv()
+    nm[1, 0].wait_recv()
+    nf[1, 0].wait_recv()
+    nf[1, 1].wait_recv()
+    sends += list(np_.values()) + list(nm.values()) + list(nf.values())
+    u_copies = {}
+    for n in range(3):
+
+        def second(i, _):
+            cols = pl.ds(pl.multiple_of(n * 512 + i * 256, 256), 256)
+            g[:, cols] = g[:, cols] + product(1 - zh, cols)
+            return 0
+
+        lax.fori_loop(0, 2, second, 0)
+        cols = pl.ds(n * 512, 512)
+        for j, d in enumerate((2, 1, 3)):
+            ty = lax.rem(y + d, 4)
+            for k in range(4):
+                rows = pl.ds(pl.multiple_of((k * 4 + ty) * 48, 16), 48)
+                us[n, j, k] = g[rows, cols].astype(BF16)
+            u_copies[n, j] = send(us.at[n, j], ur.at[n, j], u_s.at[n, j], u_r.at[n, j], device(x, y + d, z, c))
+    sends += list(u_copies.values())
 
     v_copies = {}
 
@@ -453,7 +460,7 @@
     e_copies = {}
 
     def deliver(h, buffer, landing):
-        begin, size = ((0, 64), (64, 48))[h]
+        begin, size = PARTS[h]
         for j in range(3):
             d_copies[j, h].wait_recv()
         for b in range(4):
@@ -467,7 +474,7 @@
                 buffer[i, 0:size, :] = xo[b, begin : begin + size, at : at + 128]
                 buffer[i, size : size + size // 2, 0:64] = xo[b, begin:mid, at + 128 : at + 192]
                 buffer[i, size : size + size // 2, 64:128] = xo[b, mid : begin + size, at + 128 : at + 192]
-        if h:
+        if h == 2:
             for copy in dg_copies:
                 copy.wait_recv()
             total = xg[3]
@@ -476,24 +483,25 @@
             xg[3] = total
             for a in range(2):
                 for b in range(4):
-                    buffer[a * 4 + b, 72:80, :] = jnp.zeros((8, 128), F32)
-                    buffer[a * 4 + b, 72:73, :] = xg[3, 0:1, a * 192 : a * 192 + 128]
-                    buffer[a * 4 + b, 73:74, 0:64] = xg[3, 0:1, a * 192 + 128 : a * 192 + 192]
+                    buffer[a * 4 + b, 24:32, :] = jnp.zeros((8, 128), F32)
+                    buffer[a * 4 + b, 24:25, :] = xg[3, 0:1, a * 192 : a * 192 + 128]
+                    buffer[a * 4 + b, 25:26, 0:64] = xg[3, 0:1, a * 192 + 128 : a * 192 + 192]
         for d in (4, 3, 5, 2, 6, 1, 7):
             e_copies[h, d] = send(
                 buffer.at[lax.rem(z + d, 8)], landing.at[d - 1],
                 e_s.at[h, d - 1], e_r.at[h, d - 1], device(x, y, z + d, c),
             )
 
+    deliver(0, ea, ear)
     narrow(0)
-    deliver(0, ea, ear)
     narrow(1)
     deliver(1, eb, ebr)
+    deliver(2, ec, ecr)
     narrow(2)
     sends += list(v_copies.values()) + list(e_copies.values())
 
-    for h, (buffer, landing) in enumerate(((ea, ear), (eb, ebr))):
-        begin, size = ((0, 64), (64, 48))[h]
+    for h, (buffer, landing) in enumerate(((ea, ear), (eb, ebr), (ec, ecr))):
+        begin, size = PARTS[h]
         for d in range(1, 8):
             e_copies[h, d].wait_recv()
         total = buffer[z]
@@ -503,9 +511,9 @@
         gd_out[begin : begin + size, 0:128] = total[0:size]
         gd_out[begin : begin + half, 128:192] = total[size : size + half, 0:64]
         gd_out[begin + half : begin + size, 128:192] = total[size : size + half, 64:128]
-        if h:
-            gg_out[:, 0:128] = total[72:73]
-            gg_out[:, 128:192] = total[73:74, 0:64]
+        if h == 2:
+            gg_out[:, 0:128] = total[24:25]
+            gg_out[:, 128:192] = total[25:26, 0:64]
     my_rows = pl.ds(pl.multiple_of((zl * 4 + y) * 48, 16), 48)
     for n in range(3):
         cols = pl.ds(n * 512, 512)
@@ -542,9 +550,11 @@
             jax.ShapeDtypeStruct((48, 1536), F32),
             jax.ShapeDtypeStruct((1, 192), F32),
         ),
-        in_specs=[VMEM, VMEM, VMEM, ANY, ANY],
+        in_specs=[ANY, ANY, VMEM, ANY, ANY],
         out_specs=(VMEM, VMEM, VMEM),
         scratch_shapes=[
+            pltpu.VMEM((128, 3584), BF16),
+            pltpu.VMEM((192, 256), BF16),
             pltpu.VMEM((1536, 1536), BF16),
             pltpu.VMEM((8, 2, 128, 1536), BF16),
             pltpu.VMEM((256, 192), BF16),
@@ -575,18 +585,20 @@
             pltpu.VMEM((2, 4, SUB, 384), F32),
             pltpu.VMEM((4, 8, 384), F32),
             pltpu.VMEM((3, 8, 384), F32),
-            pltpu.VMEM((8, 96, 128), F32),
-            pltpu.VMEM((7, 96, 128), F32),
-            pltpu.VMEM((8, 80, 128), F32),
-            pltpu.VMEM((7, 80, 128), F32),
+            pltpu.VMEM((8, 72, 128), F32),
+            pltpu.VMEM((7, 72, 128), F32),
+            pltpu.VMEM((8, 72, 128), F32),
+            pltpu.VMEM((7, 72, 128), F32),
+            pltpu.VMEM((8, 32, 128), F32),
+            pltpu.VMEM((7, 32, 128), F32),
             pltpu.VMEM((3, 3, 4, 48, 512), BF16),
             pltpu.VMEM((3, 3, 4, 48, 512), BF16),
             pltpu.VMEM((3, 4, 48, 512), BF16),
             pltpu.VMEM((3, 3, 48, 512), BF16),
-            dma(6),
+            dma(8),
         ]
         + pairs((3,), (4,), (), (3, 2), (), (4,), (3,), (8,), (8,), (8,), ())
-        + pairs((2,), (7,), (2,), (2,), (2,), (4, 2), (7,), (2,), (2, 2), (2, 2), (2, 2), (3, 2), (3,), (2, 7))
+        + pairs((2,), (7,), (2,), (2,), (2,), (4, 2), (7,), (2,), (2, 2), (2, 2), (2, 2), (3, 3), (3,), (3, 7))
         + pairs((3, 3), (3, 3)),
         compiler_params=pltpu.CompilerParams(
             collective_id=0, has_side_effects=True, vmem_limit_bytes=62 * 2**20

time: 171 us -> 162 us (0.947); the launches traced: 169 us -> 162 us
  Pallas kernels: 164 us -> 157 us
    pallas_call x1, Pallas kernels: 164 us -> 157 us  [local(): pl.pallas_call(whole, out_shape=(jax.ShapeDtypeStruct((112, 192), F32), j...]
where the time goes in v3:
time: 162 us
  Pallas kernels  157 us (97%)
  local copies, waits for them, and re-layouts  4.58 us (3%)
    pallas_call x1, Pallas kernels, local(): pl.pallas_call(whole, out_shape=(jax.ShapeDtypeStruct((112, 192), F32), j...  157 us
    unnamed x3, local copies, waits for them, and re-layouts  4.58 us

profile of v3, /device:TPU:1, one launch (start us, length us, event | category | flops | bytes accessed | tf_op | source)
XLA Modules:
  0.0 162.0 jit_solution(17003141112599808185)
XLA Ops:
  0.6 156.7 %shard_map.76 = (f32[112,192]{1,0:T(8,128)}, f32[48,1536]{1,0:T(8,128)}, f32[1,192]{1,0:T(1,128)}) custom-call(bf16[128,3584]{1,0:T(8,128)(2,1)} %hid.1, bf16[192,3584]{1,0:T(8,128)(2,1)} %bitcast.5, f32[1,192]{1,0:T(1,128)} %bitcast.7, bf16[1536,1536]{1,0:T(8,128)(2,1)} %wup_hbm.1, bf16[8,128,1536]{2,1,0:T(8,128)(2,1)} %bitcast.4), custom_call_target="tpu_custom_call" | custom-call | tf_op jit(solution)/shard_map/pallas_call | solution.py:546
  157.4 1.6 %copy.8 = f32[112,192]{0,1:T(8,128)} copy(f32[112,192]{1,0:T(8,128)} %get-tuple-element.9) | data formatting | bytes 172032
  159.0 1.7 %copy.11 = f32[48,1536]{1,0:T(8,128)} copy(f32[48,1536]{1,0:T(8,128)} %get-tuple-element.16) | data formatting | bytes 589824
  160.7 1.2 copy.12

commit v4 on v3

--- a/solution.py
+++ b/solution.py
@@ -12,6 +12,7 @@
 F32 = jnp.float32
 BF16 = jnp.bfloat16
 SUB = 112
+CUT = 80
 PARTS = ((0, 48), (48, 48), (96, 16))
 
 
@@ -44,6 +45,7 @@
     za_s, za_r, zb_s, zb_r, yp_s, yp_r, ym_s, ym_r, yf_s, yf_r, l_s, l_r,
     c_s, c_r, t_s, t_r, glp_s, glp_r, glm_s, glm_r, glf_s, glf_r, glc_s, glc_r, gp_s, gp_r,
     z4_s, z4_r, np_s, np_r, nm_s, nm_r, nf_s, nf_r, d_s, d_r, dg_s, dg_r, e_s, e_r, u_s, u_r, v_s, v_r,
+    wy_s, wy_r, wu_s, wu_r, wd_s, wd_r,
 ):
     x, y, z, c = coordinates()
     zh, zl = z // 4, lax.rem(z, 4)
@@ -55,9 +57,10 @@
     z4_peer = device(x, y, z + 4, c)
     up_x, down_x = device(x + 1, y, z, c), device(x - 1, y, z, c)
     up_y, down_y = device(x, y + 1, z, c), device(x, y - 1, z, c)
+    far_y = device(x, y + 2, z, c)
     up_z, down_z = device(x, y, z + s, c), device(x, y, z - s, c)
     peers = (
-        [device(x + d, y, z, c) for d in (1, 2, 3)] + [up_y, down_y, up_z, down_z, z4_peer, core_peer]
+        [device(x + d, y, z, c) for d in (1, 2, 3)] + [up_y, down_y, far_y, up_z, down_z, z4_peer, core_peer]
     )
     barrier = pltpu.get_barrier_semaphore()
     for peer in peers:
@@ -153,12 +156,14 @@
 
     def unit(zz, yy):
         zz, yy = lax.rem(zz + 16, 8), lax.rem(yy + 8, 4)
-        rows = pl.multiple_of((yy * 4 + lax.rem(zz, 4)) * SUB, 16)
-        return w.at[zz // 4, pl.ds(rows, SUB)]
-
-    my_rows = pl.ds(pl.multiple_of((y * 4 + zl) * SUB, 16), SUB)
+        return w.at[zz // 4, yy, lax.rem(zz, 4), pl.ds(0, CUT)]
+
+    def slab(zz):
+        zz = lax.rem(zz + 16, 8)
+        return w.at[zz // 4, :, lax.rem(zz, 4), pl.ds(CUT, SUB - CUT)]
+
     for i in range(4):
-        w[zh, my_rows, i * 192 : (i + 1) * 192] = xb[i]
+        w[zh, y, zl, :, i * 192 : (i + 1) * 192] = xb[i]
 
     owners = [z, z - s, z + s, z - 2 * s, z + 2 * s, z - 3 * s, z + 3 * s, z - 4 * s]
     za, zb, yp, ym, yf = {}, {}, {}, {}, {}
@@ -184,29 +189,52 @@
             there = unit(owners[k], y + 1)
             yf[k] = send(there, there, yf_s.at[k], yf_r.at[k], down_y)
 
+    rest = w.at[zh, y, zl, pl.ds(CUT, SUB - CUT)]
+    wy = [send(rest, rest, wy_s.at[i], wy_r.at[i], to) for i, to in enumerate((far_y, up_y, down_y))]
+    wu, wd = {}, {}
+
+    def climb(k):
+        if k < 4:
+            here = slab(z - s * k)
+            wu[k] = send(here, here, wu_s.at[k], wu_r.at[k], up_z)
+        if k < 3:
+            here = slab(z + s * k)
+            wd[k] = send(here, here, wd_s.at[k], wd_r.at[k], down_z)
+
     pass_on(0)
     for j, d in enumerate((2, 1, 3)):
         send_partial(j, d, 0, far)
     cotangent(x, keep)
+    for copy in wy:
+        copy.wait_recv()
+    climb(0)
     za[0].wait_recv()
     pass_on(1)
     zb[0].wait_recv()
     pass_on(2)
     forward(0)
+    wu[0].wait_recv()
+    wd[0].wait_recv()
+    climb(1)
     za[1].wait_recv()
     pass_on(3)
     zb[1].wait_recv()
     pass_on(4)
-
     forward(1)
     for j, d in enumerate((2, 1, 3)):
         n_copies[j, 0].wait_send()
         send_partial(j, d, 1, near)
+    wu[1].wait_recv()
+    wd[1].wait_recv()
+    climb(2)
     za[2].wait_recv()
     pass_on(5)
     zb[2].wait_recv()
     pass_on(6)
     forward(2)
+    wu[2].wait_recv()
+    wd[2].wait_recv()
+    climb(3)
     for j in range(3):
         n_copies[j, 0].wait_recv()
     total = own[far, :]
@@ -233,19 +261,21 @@
     sends += t_copies
     for k in range(8):
         yf[k].wait_recv()
+    wu[3].wait_recv()
     h_copy.wait_recv()
     loads[2].wait()
 
+    l_copies = []
     for half in range(2):
 
         def tile(i, _):
             cols = pl.ds(pl.multiple_of(i * 256, 256), 256)
-            value = jnp.dot(hk[...].reshape(256, 1792), w[half, :, cols], preferred_element_type=F32)
+            value = jnp.dot(hk[...].reshape(256, 1792), w[half, :, :, :, cols].reshape(1792, 256), preferred_element_type=F32)
             lp[:, half, :, cols] = value.reshape(2, 128, 256)
             return 0
 
         lax.fori_loop(0, 3, tile, 0)
-    l_copy = send(lp.at[1 - c], lx, l_s, l_r, core_peer)
+        l_copies.append(send(lp.at[1 - c, half], lx.at[half], l_s.at[half], l_r.at[half], core_peer))
 
     g_across.wait_recv()
     for j in range(3):
@@ -257,7 +287,8 @@
     own[0:128, :] = total
     for i in range(8):
         gpa[mine, :, i * 192 : (i + 1) * 192] = gb[i % 2, i // 2]
-    l_copy.wait_recv()
+    for copy in l_copies:
+        copy.wait_recv()
     for half in range(2):
         for i in range(4):
             piece_cols = pl.ds(i * 192, 192)
@@ -523,8 +554,8 @@
         for j in range(3):
             total = total + vr[n, j].astype(F32)
         gu_out[:, cols] = total
-    sends += [n_copies[j, 1] for j in range(3)] + [q_copy, l_copy]
-    for group in (za, zb, yp, ym, yf):
+    sends += [n_copies[j, 1] for j in range(3)] + [q_copy] + l_copies + wy
+    for group in (za, zb, yp, ym, yf, wu, wd):
         sends += list(group.values())
     for copy in sends:
         copy.wait_send()
@@ -561,7 +592,7 @@
             pltpu.VMEM((2, 128, 1792), BF16),
             pltpu.VMEM((4, SUB, 192), BF16),
             pltpu.VMEM((2, 4, 1, 192), F32),
-            pltpu.VMEM((2, 1792, 768), BF16),
+            pltpu.VMEM((2, 4, 4, SUB, 768), BF16),
             pltpu.VMEM((3, 256, 1536), BF16),
             pltpu.VMEM((3, 256, 1536), BF16),
             pltpu.VMEM((256, 1536), F32),
@@ -597,9 +628,9 @@
             pltpu.VMEM((3, 3, 48, 512), BF16),
             dma(8),
         ]
-        + pairs((3,), (4,), (), (3, 2), (), (4,), (3,), (8,), (8,), (8,), ())
+        + pairs((3,), (4,), (), (3, 2), (), (4,), (3,), (8,), (8,), (8,), (2,))
         + pairs((2,), (7,), (2,), (2,), (2,), (4, 2), (7,), (2,), (2, 2), (2, 2), (2, 2), (3, 3), (3,), (3, 7))
-        + pairs((3, 3), (3, 3)),
+        + pairs((3, 3), (3, 3), (3,), (4,), (3,)),
         compiler_params=pltpu.CompilerParams(
             collective_id=0, has_side_effects=True, vmem_limit_bytes=62 * 2**20
         ),

time: 162 us -> 153 us (0.944)
  Pallas kernels: 157 us -> 147 us
    pallas_call x1, Pallas kernels: 157 us -> 147 us  [local(): pl.pallas_call(whole, out_shape=(jax.ShapeDtypeStruct((112, 192), F32), j...]
where the time goes in v4:
time: 153 us; the launch traced here: 152 us
  Pallas kernels  147 us (96%)
  local copies, waits for them, and re-layouts  4.58 us (3%)
    pallas_call x1, Pallas kernels, local(): pl.pallas_call(whole, out_shape=(jax.ShapeDtypeStruct((112, 192), F32), j...  147 us
    unnamed x3, local copies, waits for them, and re-layouts  4.58 us

profile of v4, /device:TPU:1, one launch (start us, length us, event | category | flops | bytes accessed | tf_op | source)
XLA Modules:
  0.0 152.1 jit_solution(604652567860904207)
XLA Ops:
  0.6 146.9 %shard_map.76 = (f32[112,192]{1,0:T(8,128)}, f32[48,1536]{1,0:T(8,128)}, f32[1,192]{1,0:T(1,128)}) custom-call(bf16[128,3584]{1,0:T(8,128)(2,1)} %hid.1, bf16[192,3584]{1,0:T(8,128)(2,1)} %bitcast.5, f32[1,192]{1,0:T(1,128)} %bitcast.7, bf16[1536,1536]{1,0:T(8,128)(2,1)} %wup_hbm.1, bf16[8,128,1536]{2,1,0:T(8,128)(2,1)} %bitcast.4), custom_call_target="tpu_custom_call" | custom-call | tf_op jit(solution)/shard_map/pallas_call | solution.py:577
  147.5 1.6 %copy.8 = f32[112,192]{0,1:T(8,128)} copy(f32[112,192]{1,0:T(8,128)} %get-tuple-element.9) | data formatting | bytes 172032
  149.2 1.7 %copy.11 = f32[48,1536]{1,0:T(8,128)} copy(f32[48,1536]{1,0:T(8,128)} %get-tuple-element.16) | data formatting | bytes 589824
  150.9 1.2 copy.12

commit v5 on v4

--- a/solution.py
+++ b/solution.py
@@ -176,12 +176,16 @@
         if k == 0 or (k % 2 == 0 and k < 6):
             i = k // 2
             zb[i] = send(here, here, zb_s.at[i], zb_r.at[i], down_z)
+        if k == 7:
+            yf[k] = send(here, here, yf_s.at[k], yf_r.at[k], far_y)
         yp[k] = send(here, here, yp_s.at[k], yp_r.at[k], up_y)
         ym[k] = send(here, here, ym_s.at[k], ym_r.at[k], down_y)
 
     def forward(k):
         yp[k].wait_recv()
         ym[k].wait_recv()
+        if k == 7:
+            return
         if k % 2 == 0:
             there = unit(owners[k], y - 1)
             yf[k] = send(there, there, yf_s.at[k], yf_r.at[k], up_y)
@@ -452,15 +456,15 @@
     nf[1, 1].wait_recv()
     sends += list(np_.values()) + list(nm.values()) + list(nf.values())
     u_copies = {}
-    for n in range(3):
+    for n in range(6):
 
         def second(i, _):
-            cols = pl.ds(pl.multiple_of(n * 512 + i * 256, 256), 256)
+            cols = pl.ds(pl.multiple_of(n * 256 + i * 256, 256), 256)
             g[:, cols] = g[:, cols] + product(1 - zh, cols)
             return 0
 
-        lax.fori_loop(0, 2, second, 0)
-        cols = pl.ds(n * 512, 512)
+        lax.fori_loop(0, 1, second, 0)
+        cols = pl.ds(n * 256, 256)
         for j, d in enumerate((2, 1, 3)):
             ty = lax.rem(y + d, 4)
             for k in range(4):
@@ -472,7 +476,7 @@
     v_copies = {}
 
     def narrow(n):
-        cols = pl.ds(n * 512, 512)
+        cols = pl.ds(n * 256, 256)
         for j in range(3):
             u_copies[n, j].wait_recv()
         for k in range(4):
@@ -523,12 +527,15 @@
                 e_s.at[h, d - 1], e_r.at[h, d - 1], device(x, y, z + d, c),
             )
 
+    narrow(0)
     deliver(0, ea, ear)
-    narrow(0)
     narrow(1)
+    narrow(2)
     deliver(1, eb, ebr)
+    narrow(3)
     deliver(2, ec, ecr)
-    narrow(2)
+    narrow(4)
+    narrow(5)
     sends += list(v_copies.values()) + list(e_copies.values())
 
     for h, (buffer, landing) in enumerate(((ea, ear), (eb, ebr), (ec, ecr))):
@@ -546,8 +553,8 @@
             gg_out[:, 0:128] = total[24:25]
             gg_out[:, 128:192] = total[25:26, 0:64]
     my_rows = pl.ds(pl.multiple_of((zl * 4 + y) * 48, 16), 48)
-    for n in range(3):
-        cols = pl.ds(n * 512, 512)
+    for n in range(6):
+        cols = pl.ds(n * 256, 256)
         for d in (1, 2, 3):
             v_copies[n, d].wait_recv()
         total = g[my_rows, cols]
@@ -622,15 +629,15 @@
             pltpu.VMEM((7, 72, 128), F32),
             pltpu.VMEM((8, 32, 128), F32),
             pltpu.VMEM((7, 32, 128), F32),
-            pltpu.VMEM((3, 3, 4, 48, 512), BF16),
-            pltpu.VMEM((3, 3, 4, 48, 512), BF16),
-            pltpu.VMEM((3, 4, 48, 512), BF16),
-            pltpu.VMEM((3, 3, 48, 512), BF16),
+            pltpu.VMEM((6, 3, 4, 48, 256), BF16),
+            pltpu.VMEM((6, 3, 4, 48, 256), BF16),
+            pltpu.VMEM((6, 4, 48, 256), BF16),
+            pltpu.VMEM((6, 3, 48, 256), BF16),
             dma(8),
         ]
         + pairs((3,), (4,), (), (3, 2), (), (4,), (3,), (8,), (8,), (8,), (2,))
         + pairs((2,), (7,), (2,), (2,), (2,), (4, 2), (7,), (2,), (2, 2), (2, 2), (2, 2), (3, 3), (3,), (3, 7))
-        + pairs((3, 3), (3, 3), (3,), (4,), (3,)),
+        + pairs((6, 3), (6, 4), (3,), (4,), (3,)),
         compiler_params=pltpu.CompilerParams(
             collective_id=0, has_side_effects=True, vmem_limit_bytes=62 * 2**20
         ),

time: 153 us -> 152 us (level)
  no operation moved by 1% of the time
where the time goes in v5:
time: 152 us; the launch traced here: 151 us
  Pallas kernels  146 us (96%)
  local copies, waits for them, and re-layouts  4.58 us (3%)
    pallas_call x1, Pallas kernels, local(): pl.pallas_call(whole, out_shape=(jax.ShapeDtypeStruct((112, 192), F32), j...  146 us
    unnamed x3, local copies, waits for them, and re-layouts  4.58 us

profile of v5, /device:TPU:1, one launch (start us, length us, event | category | flops | bytes accessed | tf_op | source)
XLA Modules:
  0.0 151.2 jit_solution(1745155288454207706)
XLA Ops:
  0.6 146.0 %shard_map.76 = (f32[112,192]{1,0:T(8,128)}, f32[48,1536]{1,0:T(8,128)}, f32[1,192]{1,0:T(1,128)}) custom-call(bf16[128,3584]{1,0:T(8,128)(2,1)} %hid.1, bf16[192,3584]{1,0:T(8,128)(2,1)} %bitcast.5, f32[1,192]{1,0:T(1,128)} %bitcast.7, bf16[1536,1536]{1,0:T(8,128)(2,1)} %wup_hbm.1, bf16[8,128,1536]{2,1,0:T(8,128)(2,1)} %bitcast.4), custom_call_target="tpu_custom_call" | custom-call | tf_op jit(solution)/shard_map/pallas_call | solution.py:584
  146.6 1.6 %copy.8 = f32[112,192]{0,1:T(8,128)} copy(f32[112,192]{1,0:T(8,128)} %get-tuple-element.9) | data formatting | bytes 172032
  148.3 1.7 %copy.11 = f32[48,1536]{1,0:T(8,128)} copy(f32[48,1536]{1,0:T(8,128)} %get-tuple-element.16) | data formatting | bytes 589824
  150.0 1.2 copy.12
